TPU v7x, 32 devices: a whole 2x2x4 slice. The times are simulated.
32 devices in a mesh: az: 4 (over y, core), rad: 8 (over z, x).
Axes of the slice: x: 2, y: 2, z: 4, core: 2. Of those that a mesh axis runs over, the one named last changes fastest.
Arguments:
- state: float32 [8, 1, 256, 1024], P(None, None, 'rad', 'az'), may hold values from -6 to 6
- velocity: float32 [256], P('rad'), may hold values from -0.45 to 0.45
- coupling: float32 [8, 8], replicated, may hold values from -2 to 2
- diffusivity: float32 [8], replicated, may hold values from 1 to 4000, as said below
- inverse: float32 [8, 32, 32], replicated, as said below
- shifts: int32 [256], P('rad'), may hold values from 0 to 1023, as said below
Outputs:
- advected: float32 [8, 1, 256, 1024], P(None, None, 'rad', 'az')
Inputs may be any that keep to these rules, and one draw needn't show every extreme that they name: `diffusivity`: one positive diffusion number a field, spread evenly in the logarithm. inverse[f] is, up to rounding, the inverse of the 32 x 32 tridiagonal matrix with 1 + 2 diffusivity[f] on the diagonal and -diffusivity[f] beside it. `shifts`: the shift falls with radius as in a Keplerian disc: from each row to the next it drops by 0 to 9 cells, modulo 1024.
All inputs are finite; a program needn't handle non-finite values.
Results may differ from a plain program's by a relative error of at most 0.00007.
Values sent between devices are 32-bit elements; how exact they have to be, the bound alone decides.
No kernel may reach another device: no remote copies, remote signals or barrier semaphores. Data moves between devices by JAX's collectives and lax.ppermute only.
A program may use at most 64 MiB of HBM per device.

v0:
```python
import jax
import jax.numpy as jnp
from jax import lax
from jax.sharding import PartitionSpec as P

highest = lax.Precision.HIGHEST


def with_halo(block, sides, width, periodic):
    for axis, dim in sides:
        count = lax.axis_size(axis)
        forward = [(i, i + 1) for i in range(count - 1)]
        if periodic:
            forward.append((count - 1, 0))
        backward = [(target, source) for source, target in forward]
        low = lax.ppermute(
            lax.slice_in_dim(block, block.shape[dim] - width, None, axis=dim), axis, forward
        )
        high = lax.ppermute(lax.slice_in_dim(block, 0, width, axis=dim), axis, backward)
        block = jnp.concatenate([low, block, high], axis=dim)
    return block


def entering(part, axis, combine, identity, reverse):
    count = lax.axis_size(axis)
    place = lax.axis_index(axis)
    ahead = count - 1 - place if reverse else place
    gathered = jax.tree.map(lambda a: lax.all_gather(a, axis), part)
    state = jax.tree.map(lambda a, e: jnp.zeros_like(a) + jnp.asarray(e, a.dtype), part, identity)

    def one(step, state):
        source = count - 1 - step if reverse else step
        return combine(
            state, jax.tree.map(lambda a: lax.dynamic_index_in_dim(a, source, 0, False), gathered)
        )

    return lax.fori_loop(0, ahead, one, state)


def shifted(block, axis, distance):
    devices = range(lax.axis_size(axis))
    route = [((i - distance) % len(devices), i) for i in devices]
    return lax.ppermute(block, axis, route)


def chain_coefficients(diffusivity, inverse):
    last = inverse.shape[1] - 1
    return (
        diffusivity * inverse[:, 0, 0],
        diffusivity * inverse[:, last, 0],
        diffusivity * inverse[:, 0, last],
        diffusivity * inverse[:, last, last],
    )


def pivot_chain(count, coeffs):
    first_first, last_first, first_last, last_last = coeffs

    def advance(pivot, unused):
        nxt = last_last + last_first * first_last * pivot / (1.0 - first_first * pivot)
        return (nxt, pivot)

    unused_end, pivots = lax.scan(advance, jnp.zeros_like(first_first), None, length=count)
    return pivots


def compose(earlier, later):
    return (later[0] * earlier[0], later[1] + later[0][:, None, None] * earlier[1])


def per_device(state, velocity, coupling, diffusivity, inverse, shifts):
    radial_pad = with_halo(state, (("rad", 2),), 1, False)
    cycle_pad = with_halo(state, (("az", 3),), 1, True)
    east = cycle_pad[:, :, :, 2:]
    west = cycle_pad[:, :, :, :-2]
    radial_diff = radial_pad[:, :, 2:] - radial_pad[:, :, :-2]
    mixed_terms = jnp.einsum("fg,gzrp->fzrp", coupling, radial_diff, precision=highest)
    updated = state - 0.5 * velocity[None, None, :, None] * (east - west) + 0.5 * mixed_terms
    solved = jnp.einsum("frk,fzkp->fzrp", inverse, updated, precision=highest)
    block_rows = inverse.shape[1]
    heads = solved[:, :, 0]
    tails = solved[:, :, block_rows - 1]
    coeffs = chain_coefficients(diffusivity, inverse)
    first_first, last_first, first_last, last_last = coeffs
    block_count = lax.axis_size("rad")
    block_index = lax.axis_index("rad")
    pivots = pivot_chain(block_count, coeffs)
    pivot_prev = lax.dynamic_index_in_dim(pivots, block_index, 0, False)
    quotient = 1.0 - first_first * pivot_prev
    col = (slice(None), None, None)
    identity = (jnp.ones_like(first_first), jnp.zeros_like(heads))
    offset = tails + (last_first * pivot_prev / quotient)[col] * heads
    sweep_prev = entering((last_first / quotient, offset), "rad", compose, identity, False)[1]
    gamma_term = (heads + first_first[col] * sweep_prev) / quotient[col]
    front_next = entering((first_last / quotient, gamma_term), "rad", compose, identity, True)[1]
    front_now = (heads + first_first[col] * sweep_prev) / quotient[col] + (first_last / quotient)[
        col
    ] * front_next
    rear = sweep_prev + pivot_prev[col] * front_now
    first_column = inverse[:, :, 0][:, None, :, None]
    last_column = inverse[:, :, block_rows - 1][:, None, :, None]
    solution = solved + diffusivity[:, None, None, None] * (
        first_column * rear[:, :, None, :] + last_column * front_next[:, :, None, :]
    )
    az_cells = state.shape[3]
    cycle_count = lax.axis_size("az")
    cell_steps = jnp.arange(az_cells, dtype=jnp.int32)
    previous = shifted(solution, "az", 1)
    joined = jnp.concatenate([previous, solution], axis=3)
    residue = shifts % az_cells
    picks = az_cells + cell_steps[None, :] - residue[:, None]
    moved = jnp.take_along_axis(joined, jnp.broadcast_to(picks, solution.shape), axis=3)
    whole_hops = shifts // az_cells
    for bit_number in range((cycle_count - 1).bit_length()):
        hopped = shifted(moved, "az", 1 << bit_number)
        taking = whole_hops >> bit_number & 1 == 1
        moved = jnp.where(taking[None, None, :, None], hopped, moved)
    return moved


def solution(mesh):
    return jax.shard_map(
        per_device,
        mesh=mesh,
        in_specs=(P(None, None, "rad", "az"), P("rad"), P(), P(), P(), P("rad")),
        out_specs=P(None, None, "rad", "az"),
        check_vma=False,
    )
```

profile of v0, /device:TPU:1, one launch (start us, length us, event | category | flops | bytes accessed | tf_op | source)
XLA Modules:
  0.0 757.5 jit_solution(3452585392511066393)
XLA Ops:
  0.0 1.2 copy.31
  1.2 0.1 fusion.22
  1.3 0.1 collective-permute-start
  1.4 2.6 collective-permute-start.1
  4.1 1.3 collective-permute-start.2
  5.4 4.0 collective-permute-start.3
  9.4 0.2 slice_reduce_fusion
  9.6 0.1 fusion.23
  9.8 0.6 while.43
  10.4 0.6 dynamic-slice
  11.6 0.1 subtract_add_fusion
  11.7 0.1 fusion.19
  11.8 0.1 divide_dynamic-update-slice_fusion
  11.9 16.3 %all-reduce.2 = (f32[64]{0:T(128)S(1)}, f32[64]{0:T(128)S(1)}) all-reduce(f32[64]{0:T(128)S(1)} %get-tuple-element.309, f32[64]{0:T(128)S(1)} %get-tuple-element.292), channel_id=2, replica_groups=mesh['az'=4,'rad'=8] {'rad'}, use_global_device_ids=true, to_apply=%add | all-reduce | flops 128 | bytes 1024
  28.2 0.1 reshape.171
  28.3 0.1 reshape.173
  28.4 0.1 copy.43
  28.5 0.1 copy.44
  28.6 0.1 fusion.4
  28.7 0.6 fusion.9
  29.3 0.5 convolution_bitcast_fusion
  29.8 0.1 fusion.16
  29.9 24.4 %all_gather.22 = f32[8,8,1,256]{3,1,2,0:T(8,128)S(1)} all-gather(f32[1,8,1,256]{3,1,2,0:T(8,128)S(1)} %copy.36), channel_id=1, replica_groups=mesh['az'=4,'rad'=8] {'rad'}, dimensions={0}, use_global_device_ids=true | all-gather | bytes 73728 | tf_op jit(solution)/shard_map/all_gather | solution.py:28
  54.3 0.1 fusion.17
  54.4 24.3 %all-gather.1 = f32[64,1,256]{2,1,0:T(1,128)S(1)} all-gather(f32[8,1,256]{2,1,0:T(1,128)S(1)} %fusion.17), channel_id=3, replica_groups=mesh['az'=4,'rad'=8] {'rad'}, dimensions={0}, use_global_device_ids=true | all-gather | bytes 73728 | tf_op jit(solution)/shard_map/all_gather | solution.py:28
  78.7 0.9 while.42
  78.8 0.1 bitcast_add_fusion.3
  78.9 0.1 bitcast_add_fusion.3
  79.0 0.1 bitcast_add_fusion.3
  79.2 0.1 bitcast_add_fusion.3
  79.3 0.1 bitcast_add_fusion.3
  79.4 0.1 bitcast_add_fusion.3
  79.6 0.1 bitcast_add_fusion.3
  79.7 0.1 multiply_add_fusion.1
  79.8 0.1 multiply_add_fusion
  79.9 16.7 %collective-permute-start.4 = (f32[8,1,32,256]{3,2,0,1:T(8,128)S(1)}, f32[8,1,32,256]{3,2,0,1:T(8,128)S(1)}, u32[]{:S(2)}, u32[]{:S(2)}) collective-permute-start(f32[8,1,32,256]{3,2,0,1:T(8,128)S(1)} %multiply_add_fusion), channel_id=1, source_target_pairs={{24,0},{0,8},{8,16},{16,24},{25,1},{1,9},{9,17},{17,25},{26,2},{2,... | collective-permute-start | bytes 786440 | tf_op jit(solution)/shard_map/ppermute | solution.py:43
  96.7 0.1 subtract_compare_fusion
  96.8 0.1 copy.45
  96.9 3.1 collective-permute-done.4
  100.0 0.1 maximum_bitcast_fusion
  100.0 644.6 %gather_fusion = f32[65536]{0:T(1024)S(1)} fusion(f32[8,32,512]{2,1,0:T(8,128)S(1)} %maximum_bitcast_fusion, s32[65536]{0:T(1024)S(1)} %bitcast.70), kind=kCustom, calls=%fused_computation | custom fusion | bytes 1310720 | tf_op jit(solution)/shard_map/jit(take_along_axis)/gather | solution.py:112
  744.6 0.1 reshape.164
  744.7 2.5 collective-permute-start.5
  747.3 3.3 collective-permute-done.5
  750.6 0.1 broadcast_select_fusion.1
  750.7 0.7 collective-permute-start.6
  751.4 5.3 collective-permute-done.6
  756.7 0.8 broadcast_select_fusion.2
  (59 shorter events, 0.7 us)
Async XLA Ops:
  0.0 28.7 %copy-start = (f32[8,8]{1,0:T(8,128)S(1)}, f32[8,8]{1,0:T(8,128)}, u32[]{:S(2)}) copy-start(f32[8,8]{1,0:T(8,128)} %param.14) | copy-start | bytes 772
  0.0 4.1 copy-start.2
  0.0 9.4 %copy-start.1 = (f32[8,32,32]{2,1,0:T(8,128)S(1)}, f32[8,32,32]{2,1,0:T(8,128)}, u32[]{:S(2)}) copy-start(f32[8,32,32]{2,1,0:T(8,128)} %param.16) | copy-start | bytes 98308
  1.2 8.6 %copy-start.3 = (f32[8]{0:T(128)S(1)}, f32[8]{0:T(128)}, u32[]{:S(2)}) copy-start(f32[8]{0:T(128)} %param.15) | copy-start | bytes 100
  1.3 9.1 %copy-start.5 = (s32[32]{0:T(128)S(1)}, s32[32]{0:T(128)}, u32[]{:S(2)}) copy-start(s32[32]{0:T(128)} %param.17) | copy-start | bytes 388
  1.3 9.1 %copy-start.6 = (u32[32]{0:T(128)S(1)}, u32[32]{0:T(128)}, u32[]{:S(2)}) copy-start(u32[32]{0:T(128)} %constant.152) | copy-start | bytes 388
  1.3 10.6 %copy-start.4 = (f32[32]{0:T(128)S(1)}, f32[32]{0:T(128)}, u32[]{:S(2)}) copy-start(f32[32]{0:T(128)} %param.13) | copy-start | bytes 388
  1.3 27.3 %collective-permute-start = (f32[8,1,32,1]{3,0,2,1:T(8,128)S(1)}, f32[8,1,32,1]{3,0,2,1:T(8,128)S(1)}, u32[]{:S(2)}, u32[]{:S(2)}) collective-permute-start(f32[8,1,32,1]{3,0,2,1:T(8,128)S(1)} %get-tuple-element.303), channel_id=1, source_target_pairs={{8,0},{16,8},{24,16},{0,24},{9,1},{17,9},{25,17},{1,25},{10,2},{18... | collective-permute-start | bytes 3080 | tf_op jit(solution)/shard_map/ppermute | solution.py:19
  1.4 27.2 %collective-permute-start.1 = (f32[8,1,32,1]{3,0,2,1:T(8,128)S(1)}, f32[8,1,32,1]{3,0,2,1:T(8,128)S(1)}, u32[]{:S(2)}, u32[]{:S(2)}) collective-permute-start(f32[8,1,32,1]{3,0,2,1:T(8,128)S(1)} %get-tuple-element.304), channel_id=1, source_target_pairs={{0,8},{8,16},{16,24},{24,0},{1,9},{9,17},{17,25},{25,1},{2,10},{10... | collective-permute-start | bytes 3080 | tf_op jit(solution)/shard_map/ppermute | solution.py:16
  4.1 24.5 %collective-permute-start.2 = (f32[8,1,1,256]{3,2,1,0:T(1,128)S(1)}, f32[8,1,1,256]{3,2,1,0:T(1,128)S(1)}, u32[]{:S(2)}, u32[]{:S(2)}) collective-permute-start(f32[8,1,1,256]{3,2,1,0:T(1,128)S(1)} %get-tuple-element.301), channel_id=1, source_target_pairs={{1,0},{2,1},{3,2},{4,3},{5,4},{6,5},{7,6},{9,8},{10,9},{11,10},{12... | collective-permute-start | bytes 24584 | tf_op jit(solution)/shard_map/ppermute | solution.py:19
  5.4 23.2 %collective-permute-start.3 = (f32[8,1,1,256]{3,2,1,0:T(1,128)S(1)}, f32[8,1,1,256]{3,2,1,0:T(1,128)S(1)}, u32[]{:S(2)}, u32[]{:S(2)}) collective-permute-start(f32[8,1,1,256]{3,2,1,0:T(1,128)S(1)} %get-tuple-element.302), channel_id=1, source_target_pairs={{0,1},{1,2},{2,3},{3,4},{4,5},{5,6},{6,7},{8,9},{9,10},{10,11},{11... | collective-permute-start | bytes 24584 | tf_op jit(solution)/shard_map/ppermute | solution.py:16
  79.9 20.1 %collective-permute-start.4 = (f32[8,1,32,256]{3,2,0,1:T(8,128)S(1)}, f32[8,1,32,256]{3,2,0,1:T(8,128)S(1)}, u32[]{:S(2)}, u32[]{:S(2)}) collective-permute-start(f32[8,1,32,256]{3,2,0,1:T(8,128)S(1)} %multiply_add_fusion), channel_id=1, source_target_pairs={{24,0},{0,8},{8,16},{16,24},{25,1},{1,9},{9,17},{17,25},{26,2},{2,... | collective-permute-start | bytes 786440 | tf_op jit(solution)/shard_map/ppermute | solution.py:43
  744.7 5.8 collective-permute-start.5
  750.7 6.1 collective-permute-start.6
where the time goes:
time: 760 us; the launch traced here: 758 us
  local copies, waits for them, and re-layouts  648 us (85%)
  blocking collectives  65 us (9%)
  starting transfers between devices  28 us (4%)
  waiting for transfers between devices  11.7 us (2%)
    gather x2, local copies, waits for them, and re-layouts, per_device(): jnp.take_along_axis(joined, jnp.broadcast_to(picks, solution.shape), axis=3)  645 us
    all_gather x2, blocking collectives, entering(): gathered = jax.tree.map(lambda a: lax.all_gather(a, axis), part)  48.7 us
    ppermute x3, starting transfers between devices, shifted(): return lax.ppermute(block, axis, route)  20 us
    unnamed x1, blocking collectives  16.3 us
  transfers between devices with their start and end apart: 7, of which 3 were waited for; matrix products, arithmetic and copies ran while one was open for 0% of the time, Pallas kernels for 0%

commit v1 on v0

v1 whole, which is shorter than its diff:
```python
import functools

import jax
import jax.numpy as jnp
from jax import lax
from jax.experimental import pallas as pl
from jax.experimental.pallas import tpu as pltpu
from jax.sharding import PartitionSpec as P

highest = lax.Precision.HIGHEST
LANES = 128


def swapped(block, axis, bit):
    return lax.ppermute(block, axis, [(i, i ^ bit) for i in range(lax.axis_size(axis))])


def local_solve(state, velocity, coupling, inverse):
    zero_row = jnp.zeros_like(state[:, :1])
    zero_col = jnp.zeros_like(state[:, :, :1])
    radial_diff = jnp.concatenate([state[:, 1:], zero_row], 1) - jnp.concatenate(
        [zero_row, state[:, :-1]], 1
    )
    east = jnp.concatenate([state[:, :, 1:], zero_col], 2)
    west = jnp.concatenate([zero_col, state[:, :, :-1]], 2)
    half = 0.5 * velocity[None, :, None]
    mixed = jnp.einsum("fg,grp->frp", coupling, radial_diff, precision=highest)
    updated = state - half * (east - west) + 0.5 * mixed
    ghosts = [half * state[:, :, -1:], -half * state[:, :, :1]]
    blank = jnp.zeros(state.shape[:2] + (LANES - 2,), state.dtype)
    wide = jnp.concatenate([updated] + ghosts + [blank], 2)
    return jnp.einsum("frk,fkp->frp", inverse, wide, precision=highest)


def chain(head, tail, coeffs):
    a, b, c, d = [x[:, None] for x in coeffs]
    place = lax.axis_index("rad")
    levels = []
    bit = 1
    while bit < lax.axis_size("rad"):
        other = swapped(jnp.stack([head, tail]), "rad", bit)
        upper = (place & bit) != 0
        q = 1.0 - a * d
        head_1 = jnp.where(upper, other[0], head)
        tail_1 = jnp.where(upper, other[1], tail)
        head_2 = jnp.where(upper, head, other[0])
        tail_2 = jnp.where(upper, tail, other[1])
        u = (head_2 + a * tail_1) / q
        w = (tail_1 + d * head_2) / q
        levels.append((upper, u, w, a * b / q, c / q, b / q, d * c / q))
        head, tail = head_1 + c * u, tail_2 + b * w
        a, b, c, d = a + a * b * c / q, b * b / q, c * c / q, d + b * c * d / q
        bit *= 2
    left = jnp.zeros_like(head)
    right = jnp.zeros_like(head)
    for upper, u, w, ul, ur, wl, wr in reversed(levels):
        inner_right = u + ul * left + ur * right
        inner_left = w + wl * left + wr * right
        left, right = jnp.where(upper, inner_left, left), jnp.where(upper, right, inner_right)
    return left, right


def finish_kernel(count, shifts_ref, place_ref, solved_ref, forcing_ref, columns_ref, out_ref):
    fields, rows, cells = out_ref.shape
    place = place_ref[0]
    lane = lax.broadcasted_iota(jnp.int32, (fields, cells), 1)
    for r in range(rows):
        hops = lax.div(shifts_ref[r], cells)
        residue = lax.rem(shifts_ref[r], cells)
        here = lax.rem(place - hops + count, count)
        before = lax.rem(here + count - 1, count)
        after = lax.rem(here + 1, count)
        source = here ^ place
        source_low = before ^ place
        source_high = jnp.where(residue > 0, here, after) ^ place
        own = lane < cells - residue
        left = jnp.where(own, forcing_ref[source, 0, :, :cells], forcing_ref[source_low, 0, :, :cells])
        right = jnp.where(own, forcing_ref[source, 1, :, :cells], forcing_ref[source_low, 1, :, :cells])
        first = columns_ref[0, :, r : r + 1]
        last = columns_ref[1, :, r : r + 1]
        low_l = forcing_ref[source_low, 0, :, cells:]
        low_r = forcing_ref[source_low, 1, :, cells:]
        high_l = forcing_ref[source_high, 0, :, cells:]
        high_r = forcing_ref[source_high, 1, :, cells:]
        low = low_l[:, 32 + r : 33 + r] + first * low_l[:, 0:1] + last * low_r[:, 0:1]
        high = high_r[:, 32 + r : 33 + r] + first * high_l[:, 1:2] + last * high_r[:, 1:2]
        value = solved_ref[:, r, :] + first * left + last * right
        value = value + jnp.where(lane == 0, low, 0.0) + jnp.where(lane == cells - 1, high, 0.0)
        out_ref[:, r, :] = pltpu.roll(value, residue, 1)


def per_device(state, velocity, coupling, diffusivity, inverse, shifts):
    state = state[:, 0]
    fields, rows, cells = state.shape
    count = lax.axis_size("az")
    place = lax.axis_index("az")
    solved = local_solve(state, velocity, coupling, inverse)
    edge_rows = jnp.stack([state[:, 0], state[:, -1]])
    edge_mix = 0.5 * jnp.einsum("fg,egp->efp", coupling, edge_rows, precision=highest)
    edge_mix = jnp.pad(edge_mix, ((0, 0), (0, 0), (0, LANES)))
    head = diffusivity[:, None] * solved[:, 0] + edge_mix[0]
    tail = diffusivity[:, None] * solved[:, -1] - edge_mix[1]
    coeffs = (
        diffusivity * inverse[:, 0, 0],
        diffusivity * inverse[:, -1, 0],
        diffusivity * inverse[:, 0, -1],
        diffusivity * inverse[:, -1, -1],
    )
    hops = (shifts // cells)[:, None] + (
        jnp.arange(cells, dtype=jnp.int32)[None] >= cells - (shifts % cells)[:, None]
    )
    crossing = (place - hops) ^ place
    moved = solved[:, :, :cells]
    bit = 1
    while bit < count:
        moved = jnp.where(((crossing & bit) != 0)[None], swapped(moved, "az", bit), moved)
        bit *= 2
    left, right = chain(head, tail, coeffs)
    ghosts = jnp.stack([solved[:, :, cells], solved[:, :, cells + 1]])
    forcing = jnp.stack([left, right])
    forcing = jnp.concatenate(
        [
            forcing[:, :, : cells + 32],
            ghosts,
            jnp.zeros((2, fields, LANES - 32 - rows), state.dtype),
        ],
        2,
    )[None]
    bit = 1
    while bit < count:
        forcing = jnp.concatenate([forcing, swapped(forcing, "az", bit)], 0)
        bit *= 2
    columns = jnp.stack([inverse[:, :, 0], inverse[:, :, -1]])
    out = pl.pallas_call(
        functools.partial(finish_kernel, count),
        out_shape=jax.ShapeDtypeStruct((fields, rows, cells), state.dtype),
        in_specs=[pl.BlockSpec(memory_space=pltpu.SMEM)] * 2
        + [pl.BlockSpec(memory_space=pltpu.VMEM)] * 3,
        out_specs=pl.BlockSpec(memory_space=pltpu.VMEM),
    )(shifts, place[None].astype(jnp.int32), moved, forcing, columns)
    return out[:, None]


def solution(mesh):
    return jax.shard_map(
        per_device,
        mesh=mesh,
        in_specs=(P(None, None, "rad", "az"), P("rad"), P(), P(), P(), P("rad")),
        out_specs=P(None, None, "rad", "az"),
        check_vma=False,
    )
```

time: 760 us -> 44.1 us (0.06)
  local copies, waits for them, and re-layouts: 648 us -> 11.8 us
  blocking collectives: 65 us -> 0 us
  starting transfers between devices: 28 us -> 11.8 us
    gather x2 -> x0, local copies, waits for them, and re-layouts: 645 us -> none  [per_device(): jnp.take_along_axis(joined, jnp.broadcast_to(picks, solution.shape), axis=3)]
    all_gather x2 -> x0, blocking collectives: 48.7 us -> none  [entering(): gathered = jax.tree.map(lambda a: lax.all_gather(a, axis), part)]
    unnamed x1 -> x0, blocking collectives: 16.3 us -> none
    ppermute x7, starting transfers between devices: 28 us -> 11.8 us  [swapped(): lax.ppermute(block, axis, [(i, i ^ bit) for i in range(lax.axis_size(axis...]
  transfers between devices with their start and end apart: 7 -> 7, of which waited for: 3 -> 3; matrix products, arithmetic and copies ran while one was open for 0% -> 15% of each run, Pallas kernels for 0% -> 0%
where the time goes in v1:
time: 44.1 us; the launch traced here: 43.3 us
  local copies, waits for them, and re-layouts  11.8 us (27%)
  starting transfers between devices  11.8 us (27%)
  waiting for transfers between devices  8.98 us (20%)
  other arithmetic  4.85 us (11%)
  Pallas kernels  4.46 us (10%)
  matrix products  1.15 us (3%)
    ppermute x7, starting transfers between devices, swapped(): lax.ppermute(block, axis, [(i, i ^ bit) for i in range(lax.axis_size(axis...  11.8 us
    ppermute x7, waiting for transfers between devices, swapped(): lax.ppermute(block, axis, [(i, i ^ bit) for i in range(lax.axis_size(axis...  8.98 us
    pallas_call x1, Pallas kernels, per_device(): pl.pallas_call(functools.partial(finish_kernel, count), out_shape=jax.Sha...  4.46 us
    slice x2, local copies, waits for them, and re-layouts, per_device(): head = diffusivity[:, None] * solved[:, 0] + edge_mix[0]  3.54 us
    select_n x2, local copies, waits for them, and re-layouts, per_device(): jnp.where((crossing & bit != 0)[None], swapped(moved, 'az', bit), moved)  2.59 us
    select_n x2, other arithmetic, per_device(): jnp.where((crossing & bit != 0)[None], swapped(moved, 'az', bit), moved)  2.56 us
    ppermute x2, local copies, waits for them, and re-layouts, swapped(): lax.ppermute(block, axis, [(i, i ^ bit) for i in range(lax.axis_size(axis...  1.76 us
    unnamed x15, local copies, waits for them, and re-layouts  1.43 us
  transfers between devices with their start and end apart: 7, of which 3 were waited for; matrix products, arithmetic and copies ran while one was open for 15% of the time, Pallas kernels for 0%

profile of v1, /device:TPU:1, one launch (start us, length us, event | category | flops | bytes accessed | tf_op | source)
XLA Modules:
  0.0 43.3 jit_solution(13319717357629175675)
XLA Ops:
  0.0 1.2 %copy.70 = f32[8,1,32,256]{3,0,2,1:T(8,128)S(1)} copy(f32[8,1,32,256]{3,2,1,0:T(8,128)} %param.6) | data formatting | bytes 524288 | tf_op args[0]
  1.2 0.1 fusion.26
  1.4 0.2 slice_multiply_fusion.1
  1.6 0.1 pad.33.clone
  1.7 0.5 %fusion.1 = f32[8,32,256]{2,0,1:T(8,128)S(1)} fusion(f32[8,31,256]{2,0,1:T(8,128)S(1)} %get-tuple-element.44, f32[8,31,256]{2,0,1:T(8,128)S(1)} %get-tuple-element.43, f32[8,32,255]{2,0,1:T(8,128)S(1)} %get-tuple-element.42, f32[8,32,255]{2,0,1:T(8,128)S(1)} %get-tuple-element.41, f32[32]{0:T(128)S(1)} %get-tuple-element.67, f32[8,8]{1,0:T(8,128)S(1)} %copy-done, ...), kind=kOutput, calls=%fused_computation.2 | convolution fusion | flops 6684672 | bytes 1554816 | tf_op jit(solution)/shard_map/fg,grp->frp/dot_general | solution.py:27
  2.2 0.1 maximum_maximum_fusion
  2.3 0.5 %fusion.3 = f32[8,384,32]{1,2,0:T(8,128)S(1)} fusion(f32[8,32,32]{2,1,0:T(8,128)S(1)} %copy-done.1, f32[8,32,384]{2,0,1:T(8,128)S(1)} %maximum_maximum_fusion), kind=kOutput, calls=%fused_computation.8 | convolution fusion | flops 37748736 | bytes 819200 | tf_op jit(solution)/shard_map/frk,fkp->frp/dot_general | solution.py:32
  2.8 0.6 %copy.52 = f32[8,384,32]{2,0,1:T(8,128)S(1)} copy(f32[8,384,32]{1,2,0:T(8,128)S(1)} %fusion.3) | data formatting | bytes 786432 | tf_op jit(solution)/shard_map/frk,fkp->frp/dot_general | solution.py:32
  3.4 1.7 %fusion.25 = (f32[8,1,384]{1,0,2:T(8,128)}, f32[8,1,384]{1,0,2:T(8,128)S(1)}) fusion(f32[8,32,384]{1,0,2:T(8,128)S(1)} %bitcast.42), kind=kLoop, calls=%fused_computation.102 | loop fusion | bytes 49152 | tf_op jit(solution)/shard_map/slice | solution.py:101
  5.1 1.9 %copy.57 = f32[8,1,384]{2,0,1:T(8,128)S(1)} copy(f32[8,1,384]{1,0,2:T(8,128)} %get-tuple-element.37) | data formatting | bytes 24576 | tf_op jit(solution)/shard_map/slice | solution.py:101
  6.9 0.6 %copy.58 = f32[8,1,384]{2,0,1:T(8,128)S(1)} copy(f32[8,1,384]{1,0,2:T(8,128)S(1)} %get-tuple-element.38) | data formatting | bytes 24576 | tf_op jit(solution)/shard_map/slice | solution.py:102
  7.5 0.1 fusion.2
  7.7 0.1 fusion.14
  7.7 2.1 %collective-permute-start.2 = (f32[2,8,384]{2,1,0:T(8,128)S(1)}, f32[2,8,384]{2,1,0:T(8,128)S(1)}, u32[]{:S(2)}, u32[]{:S(2)}) collective-permute-start(f32[2,8,384]{2,1,0:T(8,128)S(1)} %pad_maximum_fusion.2), channel_id=1, source_target_pairs={{0,1},{1,0},{2,3},{3,2},{4,5},{5,4},{6,7},{7,6},{8,9},{9,8},{10,11... | collective-permute-start | bytes 73736 | tf_op jit(solution)/shard_map/ppermute | solution.py:15
  9.8 0.1 slice.122
  9.9 0.4 copy.53
  10.3 1.0 %collective-permute-start = (f32[8,32,256]{2,1,0:T(8,128)S(1)}, f32[8,32,256]{2,1,0:T(8,128)S(1)}, u32[]{:S(2)}, u32[]{:S(2)}) collective-permute-start(f32[8,32,256]{2,1,0:T(8,128)S(1)} %copy.53), channel_id=1, source_target_pairs={{0,8},{8,0},{16,24},{24,16},{1,9},{9,1},{17,25},{25,17},{2,10},{10... | collective-permute-start | bytes 786440 | tf_op jit(solution)/shard_map/ppermute | solution.py:15
  11.3 0.2 slice_reduce_fusion.1
  11.5 0.1 fusion.28
  11.7 0.1 and_compare_fusion.1
  11.8 0.1 multiply_add_fusion.3
  11.9 1.4 %collective-permute-start.3 = (f32[2,8,384]{2,1,0:T(8,128)S(1)}, f32[2,8,384]{2,1,0:T(8,128)S(1)}, u32[]{:S(2)}, u32[]{:S(2)}) collective-permute-start(f32[2,8,384]{2,1,0:T(8,128)S(1)} %pad_maximum_fusion.3), channel_id=1, source_target_pairs={{0,2},{1,3},{2,0},{3,1},{4,6},{5,7},{6,4},{7,5},{8,10},{9,11},{10,... | collective-permute-start | bytes 73736 | tf_op jit(solution)/shard_map/ppermute | solution.py:15
  13.3 1.4 %collective-permute-done.3 = f32[2,8,384]{2,1,0:T(8,128)S(1)} collective-permute-done((f32[2,8,384]{2,1,0:T(8,128)S(1)}, f32[2,8,384]{2,1,0:T(8,128)S(1)}, u32[]{:S(2)}, u32[]{:S(2)}) %collective-permute-start.3) | collective-permute-done | bytes 24608 | tf_op jit(solution)/shard_map/ppermute | solution.py:15
  14.7 0.1 multiply_add_fusion.1
  14.7 2.4 %collective-permute-start.4 = (f32[2,8,384]{2,1,0:T(8,128)S(1)}, f32[2,8,384]{2,1,0:T(8,128)S(1)}, u32[]{:S(2)}, u32[]{:S(2)}) collective-permute-start(f32[2,8,384]{2,1,0:T(8,128)S(1)} %pad_maximum_fusion.4), channel_id=1, source_target_pairs={{0,4},{1,5},{2,6},{3,7},{4,0},{5,1},{6,2},{7,3},{8,12},{9,13},{10,... | collective-permute-start | bytes 73736 | tf_op jit(solution)/shard_map/ppermute | solution.py:15
  17.1 0.1 pad.19.clone
  17.2 0.1 copy.49
  17.3 0.1 copy.63
  17.5 0.1 copy.64
  17.6 0.8 %collective-permute-done.4 = f32[2,8,384]{2,1,0:T(8,128)S(1)} collective-permute-done((f32[2,8,384]{2,1,0:T(8,128)S(1)}, f32[2,8,384]{2,1,0:T(8,128)S(1)}, u32[]{:S(2)}, u32[]{:S(2)}) %collective-permute-start.4) | collective-permute-done | bytes 24608 | tf_op jit(solution)/shard_map/ppermute | solution.py:15
  18.4 0.1 add_select_fusion.4
  18.5 0.1 add_select_fusion.1
  18.6 0.1 add_select_fusion
  18.6 0.1 fusion.10
  18.7 3.3 %collective-permute-start.5 = (f32[1,2,8,384]{3,2,1,0:T(8,128)S(1)}, f32[1,2,8,384]{3,2,1,0:T(8,128)S(1)}, u32[]{:S(2)}, u32[]{:S(2)}) collective-permute-start(f32[1,2,8,384]{3,2,1,0:T(8,128)S(1)} %fusion.10), channel_id=1, source_target_pairs={{0,8},{8,0},{16,24},{24,16},{1,9},{9,1},{17,25},{25,17},{2,10},{10... | collective-permute-start | bytes 73736 | tf_op jit(solution)/shard_map/ppermute | solution.py:15
  22.0 1.3 %copy.54 = f32[8,32,256]{1,0,2:T(8,128)} copy(f32[8,32,256]{2,1,0:T(8,128)S(1)} %collective-permute-done) | data formatting | bytes 524288 | tf_op jit(solution)/shard_map/ppermute | solution.py:15
  23.3 1.4 %broadcast_select_fusion = f32[8,32,256]{1,0,2:T(8,128)S(1)} fusion(f32[8,32,256]{1,0,2:T(8,128)} %copy.54, pred[32,256]{0,1:T(8,128)(4,1)S(1)} %copy.49, f32[8,32,384]{1,0,2:T(8,128)S(1)} %bitcast.45), kind=kLoop, calls=%fused_computation.5 | loop fusion | flops 65536 | bytes 794624 | tf_op jit(solution)/shard_map/jit(_where)/select_n | solution.py:116
  24.8 0.4 copy.55
  25.1 1.6 %collective-permute-start.1 = (f32[8,32,256]{2,1,0:T(8,128)S(1)}, f32[8,32,256]{2,1,0:T(8,128)S(1)}, u32[]{:S(2)}, u32[]{:S(2)}) collective-permute-start(f32[8,32,256]{2,1,0:T(8,128)S(1)} %copy.55), channel_id=1, source_target_pairs={{0,16},{8,24},{16,0},{24,8},{1,17},{9,25},{17,1},{25,9},{2,18},{10... | collective-permute-start | bytes 786440 | tf_op jit(solution)/shard_map/ppermute | solution.py:15
  26.8 0.1 collective-permute-start.6
  26.8 0.6 %pad_maximum_fusion.5.columns_ref = f32[2,8,32]{2,1,0:T(8,128)} fusion(f32[1,8,32]{2,1,0:T(8,128)S(1)} %bitcast.51, f32[1,8,32]{2,1,0:T(8,128)S(1)} %bitcast.50), kind=kLoop, calls=%fused_computation.61 | loop fusion | flops 512 | bytes 4096 | tf_op jit(solution)/shard_map/stack | solution.py:133
  27.5 0.1 copy.48
  27.6 6.8 %collective-permute-done.6 = f32[2,2,8,384]{3,2,1,0:T(8,128)S(1)} collective-permute-done((f32[2,2,8,384]{3,2,1,0:T(8,128)S(1)}, f32[2,2,8,384]{3,2,1,0:T(8,128)S(1)}, u32[]{:S(2)}, u32[]{:S(2)}) %collective-permute-start.6) | collective-permute-done | bytes 49184 | tf_op jit(solution)/shard_map/ppermute | solution.py:15
  34.4 0.6 %pad_maximum_fusion.forcing_ref = f32[4,2,8,384]{3,2,1,0:T(8,128)} fusion(f32[2,2,8,384]{3,2,1,0:T(8,128)S(1)} %collective-permute-done.6, f32[1,2,8,384]{3,2,1,0:T(8,128)S(1)} %collective-permute-done.5, f32[1,2,8,384]{3,2,1,0:T(8,128)S(1)} %fusion.10), kind=kLoop, calls=%fused_computation.16 | loop fusion | flops 49152 | bytes 196608 | tf_op jit(solution)/shard_map/concatenate | solution.py:131
  35.0 0.4 copy.56
  35.4 1.1 %broadcast_select_fusion.1 = f32[8,32,256]{1,0,2:T(8,128)} fusion(f32[8,32,256]{1,0,2:T(8,128)S(1)} %copy.56, f32[8,32,256]{1,0,2:T(8,128)S(1)} %broadcast_select_fusion, pred[32,256]{0,1:T(8,128)(4,1)S(1)} %copy.48), kind=kLoop, calls=%fused_computation.6 | loop fusion | flops 65536 | bytes 794624 | tf_op jit(solution)/shard_map/jit(_where)/select_n | solution.py:116
  36.6 2.2 %copy.61.solved_ref = f32[8,32,256]{2,1,0:T(8,128)} copy(f32[8,32,256]{1,0,2:T(8,128)} %broadcast_select_fusion.1) | data formatting | bytes 524288 | tf_op jit(solution)/shard_map/jit(_where)/select_n | solution.py:116
  38.8 4.5 %shard_map.64 = f32[8,32,256]{2,1,0:T(8,128)} custom-call(s32[32]{0:T(128)} %shifts_ref.1, s32[1]{0:T(128)} %bitcast.place_ref, f32[8,32,256]{2,1,0:T(8,128)} %copy.61.solved_ref, f32[4,2,8,384]{3,2,1,0:T(8,128)} %pad_maximum_fusion.forcing_ref, f32[2,8,32]{2,1,0:T(8,128)} %pad_maximum_fusion.5.columns_ref), custom_call_target="tpu_custom_call" | custom-call | tf_op jit(solution)/shard_map/pallas_call | solution.py:134
  (33 shorter events, 0.2 us)
Async XLA Ops:
  0.0 1.7 %copy-start = (f32[8,8]{1,0:T(8,128)S(1)}, f32[8,8]{1,0:T(8,128)}, u32[]{:S(2)}) copy-start(f32[8,8]{1,0:T(8,128)} %param.8) | copy-start | bytes 772
  0.0 1.7 %copy-start.2 = (f32[8,1,32,256]{3,2,1,0:T(8,128)S(1)}, f32[8,1,32,256]{3,2,1,0:T(8,128)}, u32[]{:S(2)}) copy-start(f32[8,1,32,256]{3,2,1,0:T(8,128)} %param.6) | copy-start | bytes 786436
  0.0 1.4 %copy-start.5 = (f32[32]{0:T(128)S(1)}, f32[32]{0:T(128)}, u32[]{:S(2)}) copy-start(f32[32]{0:T(128)} %param.7) | copy-start | bytes 388
  1.4 0.9 %copy-start.1 = (f32[8,32,32]{2,1,0:T(8,128)S(1)}, f32[8,32,32]{2,1,0:T(8,128)}, u32[]{:S(2)}) copy-start(f32[8,32,32]{2,1,0:T(8,128)} %param.10) | copy-start | bytes 98308
  5.1 2.6 %copy-start.3 = (f32[8]{0:T(128)S(1)}, f32[8]{0:T(128)}, u32[]{:S(2)}) copy-start(f32[8]{0:T(128)} %param.9) | copy-start | bytes 100
  7.7 3.9 %copy-start.4 = (s32[32]{0:T(128)S(1)}, s32[32]{0:T(128)}, u32[]{:S(2)}) copy-start(s32[32]{0:T(128)} %shifts_ref.1) | copy-start | bytes 388
  7.7 4.1 %collective-permute-start.2 = (f32[2,8,384]{2,1,0:T(8,128)S(1)}, f32[2,8,384]{2,1,0:T(8,128)S(1)}, u32[]{:S(2)}, u32[]{:S(2)}) collective-permute-start(f32[2,8,384]{2,1,0:T(8,128)S(1)} %pad_maximum_fusion.2), channel_id=1, source_target_pairs={{0,1},{1,0},{2,3},{3,2},{4,5},{5,4},{6,7},{7,6},{8,9},{9,8},{10,11... | collective-permute-start | bytes 73736 | tf_op jit(solution)/shard_map/ppermute | solution.py:15
  10.3 11.7 %collective-permute-start = (f32[8,32,256]{2,1,0:T(8,128)S(1)}, f32[8,32,256]{2,1,0:T(8,128)S(1)}, u32[]{:S(2)}, u32[]{:S(2)}) collective-permute-start(f32[8,32,256]{2,1,0:T(8,128)S(1)} %copy.53), channel_id=1, source_target_pairs={{0,8},{8,0},{16,24},{24,16},{1,9},{9,1},{17,25},{25,17},{2,10},{10... | collective-permute-start | bytes 786440 | tf_op jit(solution)/shard_map/ppermute | solution.py:15
  11.9 2.7 %collective-permute-start.3 = (f32[2,8,384]{2,1,0:T(8,128)S(1)}, f32[2,8,384]{2,1,0:T(8,128)S(1)}, u32[]{:S(2)}, u32[]{:S(2)}) collective-permute-start(f32[2,8,384]{2,1,0:T(8,128)S(1)} %pad_maximum_fusion.3), channel_id=1, source_target_pairs={{0,2},{1,3},{2,0},{3,1},{4,6},{5,7},{6,4},{7,5},{8,10},{9,11},{10,... | collective-permute-start | bytes 73736 | tf_op jit(solution)/shard_map/ppermute | solution.py:15
  14.7 3.6 %collective-permute-start.4 = (f32[2,8,384]{2,1,0:T(8,128)S(1)}, f32[2,8,384]{2,1,0:T(8,128)S(1)}, u32[]{:S(2)}, u32[]{:S(2)}) collective-permute-start(f32[2,8,384]{2,1,0:T(8,128)S(1)} %pad_maximum_fusion.4), channel_id=1, source_target_pairs={{0,4},{1,5},{2,6},{3,7},{4,0},{5,1},{6,2},{7,3},{8,12},{9,13},{10,... | collective-permute-start | bytes 73736 | tf_op jit(solution)/shard_map/ppermute | solution.py:15
  18.7 8.0 %collective-permute-start.5 = (f32[1,2,8,384]{3,2,1,0:T(8,128)S(1)}, f32[1,2,8,384]{3,2,1,0:T(8,128)S(1)}, u32[]{:S(2)}, u32[]{:S(2)}) collective-permute-start(f32[1,2,8,384]{3,2,1,0:T(8,128)S(1)} %fusion.10), channel_id=1, source_target_pairs={{0,8},{8,0},{16,24},{24,16},{1,9},{9,1},{17,25},{25,17},{2,10},{10... | collective-permute-start | bytes 73736 | tf_op jit(solution)/shard_map/ppermute | solution.py:15
  25.1 9.9 %collective-permute-start.1 = (f32[8,32,256]{2,1,0:T(8,128)S(1)}, f32[8,32,256]{2,1,0:T(8,128)S(1)}, u32[]{:S(2)}, u32[]{:S(2)}) collective-permute-start(f32[8,32,256]{2,1,0:T(8,128)S(1)} %copy.55), channel_id=1, source_target_pairs={{0,16},{8,24},{16,0},{24,8},{1,17},{9,25},{17,1},{25,9},{2,18},{10... | collective-permute-start | bytes 786440 | tf_op jit(solution)/shard_map/ppermute | solution.py:15
  26.8 7.6 %collective-permute-start.6 = (f32[2,2,8,384]{3,2,1,0:T(8,128)S(1)}, f32[2,2,8,384]{3,2,1,0:T(8,128)S(1)}, u32[]{:S(2)}, u32[]{:S(2)}) collective-permute-start(f32[2,2,8,384]{3,2,1,0:T(8,128)S(1)} %pad_maximum_fusion.1), channel_id=1, source_target_pairs={{0,16},{8,24},{16,0},{24,8},{1,17},{9,25},{17,1},{25,9},{2,18},{10... | collective-permute-start | bytes 147464 | tf_op jit(solution)/shard_map/ppermute | solution.py:15

commit v2 on v1

v2 whole, which is shorter than its diff:
```python
import functools

import jax
import jax.numpy as jnp
from jax import lax
from jax.experimental import pallas as pl
from jax.experimental.pallas import tpu as pltpu
from jax.sharding import PartitionSpec as P

highest = lax.Precision.HIGHEST
f32 = jnp.float32
LANES = 128
SMEM = pl.BlockSpec(memory_space=pltpu.SMEM)
VMEM = pl.BlockSpec(memory_space=pltpu.VMEM)
ANY = pl.BlockSpec(memory_space=pl.ANY)


def in_vmem(x):
    return pltpu.with_memory_space_constraint(x, pltpu.VMEM)


def iota(shape, dim):
    return lax.broadcasted_iota(jnp.int32, shape, dim)


def log2(number):
    assert number & (number - 1) == 0
    return number.bit_length() - 1


def swapped(block, axis, bit):
    return lax.ppermute(block, axis, [(i, i ^ bit) for i in range(lax.axis_size(axis))])


def tile(x, j):
    return x[:, j * LANES : (j + 1) * LANES]


def as_column(row):
    n = row.shape[1]
    same = iota((n, n), 0) == iota((n, n), 1)
    return jnp.sum(jnp.where(same, jnp.broadcast_to(row, (n, n)), 0.0), axis=1, keepdims=True)


def level_coefficients(first, last, count, place):
    fields = first.shape[0]
    wide = (fields, LANES)
    a = jnp.broadcast_to(first[:, :1], wide)
    b = jnp.broadcast_to(last[:, :1], wide)
    c = jnp.broadcast_to(first[:, -1:], wide)
    d = jnp.broadcast_to(last[:, -1:], wide)
    one, none = jnp.ones(wide, f32), jnp.zeros(wide, f32)
    left_l, left_r, right_l, right_r = one, none, none, one
    found = []
    bit = 1
    while bit < count:
        side = iota(wide, 0) * 0 + (place & bit)
        upper = side != 0
        q = 1.0 / (1.0 - a * d)
        own = q * jnp.where(upper, d, a)
        felt_l = jnp.where(upper, left_l, left_r)
        felt_r = jnp.where(upper, right_l, right_r)
        if 2 * bit == count:
            found += [felt_l * q, felt_l * own, felt_r * q, felt_r * own]
            break
        found += [q, own, q * jnp.where(upper, a, d), felt_l, felt_r, b, c]
        via_l = jnp.where(upper, b * q, a * b * q)
        via_r = jnp.where(upper, c * d * q, c * q)
        left_l, left_r = (
            jnp.where(upper, none, left_l) + felt_l * via_l,
            jnp.where(upper, left_r, none) + felt_l * via_r,
        )
        right_l, right_r = (
            jnp.where(upper, none, right_l) + felt_r * via_l,
            jnp.where(upper, right_r, none) + felt_r * via_r,
        )
        a, b, c, d = a + a * b * c * q, b * b * q, c * c * q, d + b * c * d * q
        bit *= 2
    return found


def offsets_kernel(
    count, state_hbm, inverse_hbm, velocity_hbm, coupling_hbm, diffusivity_hbm,
    out_ref, coeffs_ref, state_ref, inverse_ref, velocity_ref, coupling_ref, diffusivity_ref, sems,
):
    copies = [
        pltpu.make_async_copy(source, target, sems.at[i])
        for i, (source, target) in enumerate(
            (
                (inverse_hbm, inverse_ref),
                (velocity_hbm, velocity_ref),
                (coupling_hbm, coupling_ref),
                (diffusivity_hbm, diffusivity_ref),
                (state_hbm, state_ref),
            )
        )
    ]
    for copy in copies:
        copy.start()
    for copy in copies[:4]:
        copy.wait()
    fields, rows, cells = state_ref.shape
    span = fields * rows
    diffusivity = as_column(diffusivity_ref[...])
    first = diffusivity * inverse_ref[:, 0, :]
    last = diffusivity * inverse_ref[:, rows - 1, :]
    for i, x in enumerate(level_coefficients(first, last, count, lax.axis_index("rad"))):
        coeffs_ref[i] = x
    first = jnp.concatenate([first] * fields, axis=1)
    last = jnp.concatenate([last] * fields, axis=1)
    speed = jnp.concatenate([jnp.broadcast_to(velocity_ref[...], (fields, rows))] * fields, axis=1)
    lane = iota((fields, span), 1)
    row = lane & (rows - 1)
    group = lane >> log2(rows)
    own = group == iota((fields, span), 0)
    mix = jnp.zeros((fields, span), f32)
    for g in range(fields):
        mix = jnp.where(group == g, coupling_ref[:, g : g + 1], mix)
    weights = []
    drift = []
    for vector, below, above in ((first, 1.0, 0.0), (last, 0.0, 1.0)):
        lower = jnp.where(row == 0, below, pltpu.roll(vector, 1, 1))
        upper = jnp.where(row == rows - 1, above, pltpu.roll(vector, span - 1, 1))
        weights.append(jnp.where(own, vector, 0.0) + 0.5 * mix * (lower - upper))
        drift.append(jnp.where(own, 0.5 * speed * vector, 0.0))
    table = jnp.concatenate(weights + drift, axis=0)
    copies[4].wait()
    sums = jnp.dot(
        table,
        state_ref[...].reshape(span, cells),
        precision=highest,
        preferred_element_type=f32,
    )
    blank = jnp.zeros((2 * fields, LANES), f32)
    main = jnp.concatenate([sums[: 2 * fields], blank], axis=1)
    side = jnp.concatenate([sums[2 * fields :], blank], axis=1)
    width = cells + LANES
    total = main + pltpu.roll(side, 1, 1) - pltpu.roll(side, width - 1, 1)
    for e in range(2):
        for j in range(width // LANES):
            out_ref[e, j] = tile(total[e * fields : (e + 1) * fields], j)


def solve_kernel(
    count, coupling_ref, state_ref, velocity_ref, inverse_ref,
    out_ref, columns_ref, diff_ref, updated_ref, table_ref,
):
    fields, rows, cells = state_ref.shape
    span = fields * rows
    width = cells + LANES
    row = iota((rows, cells), 0)
    half = 0.5 * as_column(velocity_ref[...])
    for g in range(fields):
        block = state_ref[g]
        upper = jnp.where(row == rows - 1, 0.0, pltpu.roll(block, rows - 1, 0))
        lower = jnp.where(row == 0, 0.0, pltpu.roll(block, 1, 0))
        diff_ref[g] = 0.5 * (upper - lower)
        padded = jnp.concatenate([block, jnp.zeros((rows, LANES), f32)], axis=1)
        updated_ref[g * rows : (g + 1) * rows] = padded + half * (
            pltpu.roll(padded, 1, 1) - pltpu.roll(padded, width - 1, 1)
        )
        pad = [jnp.zeros((rows, rows), f32)] * fields
        pad[g] = inverse_ref[g]
        placed = jnp.concatenate(pad, axis=1)
        for j in range(span // LANES):
            table_ref[j, pl.ds(g, rows, stride=fields), :] = tile(placed, j)
    for f in range(fields):
        total = updated_ref[f * rows : (f + 1) * rows, :cells]
        for g in range(fields):
            total = total + coupling_ref[f, g] * diff_ref[g]
        updated_ref[f * rows : (f + 1) * rows, :cells] = total
    solved = jnp.dot(
        jnp.concatenate([table_ref[j] for j in range(span // LANES)], axis=1),
        updated_ref[...],
        precision=highest,
        preferred_element_type=f32,
    )
    lane = iota((fields, LANES), 1)
    ghosts = jnp.zeros((fields, LANES), f32)
    for r in range(rows):
        block = solved[r * fields : (r + 1) * fields]
        out_ref[r, 0] = tile(block, 0)
        out_ref[r, 1] = tile(block, 1)
        edge = tile(block, 2)
        ghosts = jnp.where(lane == r, pltpu.roll(edge, r, 1), ghosts)
        ghosts = jnp.where(lane == rows + r, pltpu.roll(edge, rows + r + 1, 1), ghosts)
        columns_ref[0, r] = jnp.broadcast_to(inverse_ref[:, r, :1], (fields, LANES))
        columns_ref[1, r] = jnp.broadcast_to(inverse_ref[:, r, rows - 1 :], (fields, LANES))
    place = lax.axis_index("az")
    for at in range(count * 2 * rows // LANES):
        for part in range(LANES // (2 * rows)):
            mine = iota((fields, LANES), 0) * 0 + place == at * (LANES // (2 * rows)) + part
            moved = pltpu.roll(ghosts, part * 2 * rows, 1) if part else ghosts
            value = jnp.where(mine, moved, 0.0)
            total = value if part == 0 else total + value
        out_ref[rows + at // 2, at % 2] = total


def masks(shift, cells, place, bit):
    hops = shift >> log2(cells)
    residue = shift & (cells - 1)
    near = ((place - hops) ^ place) & bit
    far = ((place - hops - 1) ^ place) & bit
    lane = iota((8, LANES), 1)
    return [jnp.where(lane + j * LANES < cells - residue, near, far) != 0 for j in range(2)]


def select_kernel(bit, shifts_ref, kept_ref, came_ref, out_ref):
    rows = shifts_ref.shape[0]
    place = lax.axis_index("az")
    for r in range(rows):
        take = masks(shifts_ref[r], 2 * LANES, place, bit)
        for j in range(2):
            out_ref[r, j] = jnp.where(take[j], came_ref[r, j], kept_ref[r, j])
    out_ref[rows:] = kept_ref[rows:] + came_ref[rows:]


def turned(value, residue):
    amount = residue & (LANES - 1)
    low = iota(value[0].shape, 1) < amount
    turn = [pltpu.roll(x, amount, 1) for x in value]
    return [jnp.where(low, turn[1], turn[0]), jnp.where(low, turn[0], turn[1])]


def rotate_kernel(count, bit, shifts_ref, kept_ref, came_ref, out_ref, ghosts_ref):
    rows, tiles, fields, lanes = out_ref.shape
    cells = tiles * lanes
    per_tile = lanes // (2 * rows)
    place = lax.axis_index("az")
    lane = iota((fields, lanes), 1)
    for at in range(count * 2 * rows // lanes):
        ghosts_ref[at] = kept_ref[rows + at // 2, at % 2] + came_ref[rows + at // 2, at % 2]
    for r in range(rows):
        shift = shifts_ref[r]
        hops = shift >> log2(cells)
        residue = shift & (cells - 1)
        take = masks(shift, cells, place, bit)
        value = [jnp.where(take[j], came_ref[r, j], kept_ref[r, j]) for j in range(2)]
        here = (place - hops) & (count - 1)
        before = (here - 1) & (count - 1)
        after = jnp.where(residue > 0, here, (here + 1) & (count - 1))
        low_at = (before & (per_tile - 1)) * 2 * rows + r
        high_at = (after & (per_tile - 1)) * 2 * rows + rows + r
        low = pltpu.roll(ghosts_ref[before >> log2(per_tile)], (lanes - low_at) & (lanes - 1), 1)
        high = pltpu.roll(ghosts_ref[after >> log2(per_tile)], lanes - 1 - high_at, 1)
        value[0] = value[0] + jnp.where(lane == 0, low, 0.0)
        value[1] = value[1] + jnp.where(lane == lanes - 1, high, 0.0)
        value = turned(value, residue)
        swap = residue >> log2(lanes)
        out_ref[r, swap] = value[0]
        out_ref[r, 1 - swap] = value[1]


def finish_kernel(count, parts, shifts_ref, columns_ref, rotated_ref, *rest):
    out_hbm, forcing_ref, total_ref, sems = rest[parts:]
    rows, tiles, fields, lanes = rotated_ref.shape
    cells = tiles * lanes
    chunk = 8
    at = 0
    place = lax.axis_index("az")
    lane = iota((fields, lanes), 1)
    for part in rest[:parts]:
        forcing_ref[at : at + part.shape[0]] = part[...]
        at += part.shape[0]
    for m in range(count):
        before = (((place ^ m) - 1) & (count - 1)) ^ place
        after = (((place ^ m) + 1) & (count - 1)) ^ place
        for e in range(2):
            forcing_ref[m, e, 0] += jnp.where(lane == 0, forcing_ref[before, e, tiles], 0.0)
            forcing_ref[m, e, 1] += jnp.where(lane == lanes - 1, forcing_ref[after, e, tiles], 0.0)
    copies = []
    for r in range(rows):
        shift = shifts_ref[r]
        hops = shift >> log2(cells)
        residue = shift & (cells - 1)
        here = (place - hops) & (count - 1)
        source = here ^ place
        source_low = ((here - 1) & (count - 1)) ^ place
        value = []
        for j in range(2):
            near = lane + j * lanes < cells - residue
            left = jnp.where(near, forcing_ref[source, 0, j], forcing_ref[source_low, 0, j])
            right = jnp.where(near, forcing_ref[source, 1, j], forcing_ref[source_low, 1, j])
            value.append(columns_ref[0, r] * left + columns_ref[1, r] * right)
        value = turned(value, residue)
        swap = residue >> log2(lanes)
        for j, x in ((swap, value[0]), (1 - swap, value[1])):
            total_ref[r // chunk, j, pl.ds(r % chunk, fields, stride=chunk), :] = x + rotated_ref[r, j]
        if r % chunk == chunk - 1:
            for j in range(2):
                copies.append(
                    pltpu.make_async_copy(
                        total_ref.at[r // chunk, j].reshape(fields, chunk, lanes),
                        out_hbm.at[:, pl.ds(r + 1 - chunk, chunk), pl.ds(j * lanes, lanes)],
                        sems.at[r // chunk, j],
                    )
                )
                copies[-1].start()
    for copy in copies:
        copy.wait()


def chain(offsets, coeffs):
    place = lax.axis_index("rad")
    count = lax.axis_size("rad")
    head, tail = offsets[0], offsets[1]
    left = right = None
    bit = 1
    at = 0
    while 2 * bit < count:
        upper = (place & bit) != 0
        q, own, other_scale, felt_l, felt_r, b, c = [coeffs[at + i] for i in range(7)]
        at += 7
        other = swapped(jnp.stack([head, tail]), "rad", bit)
        meeting = jnp.where(upper, other[1], other[0])
        facing = jnp.where(upper, head, tail)
        inner = q * meeting + own * facing
        partner = q * facing + other_scale * meeting
        left = felt_l * inner if left is None else left + felt_l * inner
        right = felt_r * inner if right is None else right + felt_r * inner
        head = jnp.where(upper, other[0], head) + c * jnp.where(upper, partner, inner)
        tail = jnp.where(upper, tail, other[1]) + b * jnp.where(upper, inner, partner)
        bit *= 2
    upper = (place & bit) != 0
    facing = jnp.where(upper, head, tail)
    meeting = swapped(facing, "rad", bit)
    return jnp.stack(
        [
            left + coeffs[at] * meeting + coeffs[at + 1] * facing,
            right + coeffs[at + 2] * meeting + coeffs[at + 3] * facing,
        ]
    )


def per_device(state, velocity, coupling, diffusivity, inverse, shifts):
    state = state[:, 0]
    fields, rows, cells = state.shape
    tiles = cells // LANES
    assert tiles == 2 and fields == 8 and 2 * rows <= LANES
    count = lax.axis_size("az")
    levels = log2(lax.axis_size("rad"))
    offsets, coeffs, state_near, inverse_near = pl.pallas_call(
        functools.partial(offsets_kernel, lax.axis_size("rad")),
        out_shape=[
            pltpu.VMEM((2, tiles + 1, fields, LANES), f32),
            pltpu.VMEM((7 * levels - 3, fields, LANES), f32),
            pltpu.VMEM(state.shape, f32),
            pltpu.VMEM(inverse.shape, f32),
        ],
        in_specs=[ANY] * 5,
        out_specs=[VMEM] * 4,
        scratch_shapes=[
            pltpu.VMEM((1, rows), f32),
            pltpu.VMEM((fields, fields), f32),
            pltpu.VMEM((1, fields), f32),
            pltpu.SemaphoreType.DMA((5,)),
        ],
        name="offsets",
    )(state, inverse, velocity[None], coupling, diffusivity[None])
    spare = count * 2 * rows // cells
    solved, columns = pl.pallas_call(
        functools.partial(solve_kernel, count),
        out_shape=[
            pltpu.VMEM((rows + spare, tiles, fields, LANES), f32),
            pltpu.VMEM((2, rows, fields, LANES), f32),
        ],
        in_specs=[SMEM] + [VMEM] * 3,
        out_specs=[VMEM] * 2,
        scratch_shapes=[
            pltpu.VMEM((fields, rows, cells), f32),
            pltpu.VMEM((fields * rows, cells + LANES), f32),
            pltpu.VMEM((fields * rows // LANES, fields * rows, LANES), f32),
        ],
        name="solve",
    )(coupling, in_vmem(state_near), velocity[None], in_vmem(inverse_near))
    kept = solved
    bit = 1
    while 2 * bit < count:
        kept = pl.pallas_call(
            functools.partial(select_kernel, bit),
            out_shape=pltpu.VMEM(solved.shape, f32),
            in_specs=[SMEM] + [VMEM] * 2,
            out_specs=VMEM,
            name="select",
        )(shifts, in_vmem(kept), in_vmem(swapped(kept, "az", bit)))
        bit *= 2
    rotated = pl.pallas_call(
        functools.partial(rotate_kernel, count, bit),
        out_shape=pltpu.VMEM((rows, tiles, fields, LANES), f32),
        in_specs=[SMEM] + [VMEM] * 2,
        out_specs=VMEM,
        scratch_shapes=[pltpu.VMEM((count * 2 * rows // LANES, fields, LANES), f32)],
        name="rotate",
    )(shifts, in_vmem(kept), in_vmem(swapped(kept, "az", bit)))
    forcing = chain(offsets, coeffs)
    parts = [forcing[None]]
    bit = 1
    while bit < count:
        parts.append(swapped(jnp.concatenate(parts, 0), "az", bit))
        bit *= 2
    out = pl.pallas_call(
        functools.partial(finish_kernel, count, len(parts)),
        out_shape=jax.ShapeDtypeStruct(state.shape, f32),
        in_specs=[SMEM] + [VMEM] * (2 + len(parts)),
        out_specs=ANY,
        scratch_shapes=[
            pltpu.VMEM((count, 2, tiles + 1, fields, LANES), f32),
            pltpu.VMEM((rows // 8, tiles, 8 * fields, LANES), f32),
            pltpu.SemaphoreType.DMA((rows // 8, tiles)),
        ],
        name="finish",
    )(shifts, in_vmem(columns), in_vmem(rotated), *map(in_vmem, parts))
    return out[:, None]


def solution(mesh):
    return jax.shard_map(
        per_device,
        mesh=mesh,
        in_specs=(P(None, None, "rad", "az"), P("rad"), P(), P(), P(), P("rad")),
        out_specs=P(None, None, "rad", "az"),
        check_vma=False,
    )
```

time: 44.1 us -> 30.1 us (0.68)
  the two profiles are of different devices: /device:TPU:1 before, /device:TPU:0 now
where the time goes in v2:
time: 30.1 us; the launch traced here: 29.9 us
  waiting for transfers between devices  12.1 us (40%)
  starting transfers between devices  10.4 us (35%)
  Pallas kernels  7.2 us (24%)
    ppermute x7, waiting for transfers between devices, swapped(): lax.ppermute(block, axis, [(i, i ^ bit) for i in range(lax.axis_size(axis...  12.1 us
    ppermute x7, starting transfers between devices, swapped(): lax.ppermute(block, axis, [(i, i ^ bit) for i in range(lax.axis_size(axis...  10.4 us
    pallas_call x1, Pallas kernels, per_device(): pl.pallas_call(functools.partial(solve_kernel, count), out_shape=[pltpu.V...  2.12 us
    pallas_call x1, Pallas kernels, per_device(): pl.pallas_call(functools.partial(finish_kernel, count, len(parts)), out_s...  1.72 us
    pallas_call x1, Pallas kernels, per_device(): pl.pallas_call(functools.partial(offsets_kernel, lax.axis_size('rad')), o...  1.5 us
    pallas_call x1, Pallas kernels, per_device(): pl.pallas_call(functools.partial(rotate_kernel, count, bit), out_shape=pl...  1.11 us
    pallas_call x1, Pallas kernels, per_device(): pl.pallas_call(functools.partial(select_kernel, bit), out_shape=pltpu.VME...  0.76 us
  transfers between devices with their start and end apart: 7, of which 5 were waited for; matrix products, arithmetic and copies ran while one was open for 0% of the time, Pallas kernels for 11%

profile of v2, /device:TPU:0, one launch (start us, length us, event | category | flops | bytes accessed | tf_op | source)
XLA Modules:
  0.0 29.9 jit_solution(5851537961132939503)
XLA Ops:
  0.0 1.5 %offsets.1 = (f32[2,3,8,128]{3,2,1,0:T(8,128)S(1)}, f32[18,8,128]{2,1,0:T(8,128)S(1)}, f32[8,32,256]{2,1,0:T(8,128)S(1)}, f32[8,32,32]{2,1,0:T(8,128)S(1)}) custom-call(f32[8,32,256]{2,1,0:T(8,128)} %bitcast.106, f32[8,32,32]{2,1,0:T(8,128)} %inverse_hbm.1, f32[1,32]{1,0:T(1,128)} %bitcast.107, f32[8,8]{1,0:T(8,128)} %coupling_ref.1, f32[1,8]{1,0:T(1,128)} %bitcast.109), custom_call_target="tpu_custom_call" | custom-call | tf_op jit(solution)/shard_map/offsets/pallas_call | solution.py:342
  1.5 3.0 %collective-permute-start.2 = (f32[2,3,8,128]{3,2,1,0:T(8,128)S(1)}, f32[2,3,8,128]{3,2,1,0:T(8,128)S(1)}, u32[]{:S(2)}, u32[]{:S(2)}) collective-permute-start(f32[2,3,8,128]{3,2,1,0:T(8,128)S(1)} %get-tuple-element.16), channel_id=1, source_target_pairs={{0,1},{1,0},{2,3},{3,2},{4,5},{5,4},{6,7},{7,6},{8,9},{9,8},{10,11... | collective-permute-start | bytes 73736 | tf_op jit(solution)/shard_map/ppermute | solution.py:32
  4.5 1.8 %collective-permute-done.2 = f32[2,3,8,128]{3,2,1,0:T(8,128)S(1)} collective-permute-done((f32[2,3,8,128]{3,2,1,0:T(8,128)S(1)}, f32[2,3,8,128]{3,2,1,0:T(8,128)S(1)}, u32[]{:S(2)}, u32[]{:S(2)}) %collective-permute-start.2) | collective-permute-done | bytes 24608 | tf_op jit(solution)/shard_map/ppermute | solution.py:32
  6.4 2.2 %collective-permute-start.3 = (f32[2,3,8,128]{3,2,1,0:T(8,128)S(1)}, f32[2,3,8,128]{3,2,1,0:T(8,128)S(1)}, u32[]{:S(2)}, u32[]{:S(2)}) collective-permute-start(f32[2,3,8,128]{3,2,1,0:T(8,128)S(1)} %pad_maximum_fusion.1), channel_id=1, source_target_pairs={{0,2},{1,3},{2,0},{3,1},{4,6},{5,7},{6,4},{7,5},{8,10},{9,11},{10,... | collective-permute-start | bytes 73736 | tf_op jit(solution)/shard_map/ppermute | solution.py:32
  8.5 1.8 %collective-permute-done.3 = f32[2,3,8,128]{3,2,1,0:T(8,128)S(1)} collective-permute-done((f32[2,3,8,128]{3,2,1,0:T(8,128)S(1)}, f32[2,3,8,128]{3,2,1,0:T(8,128)S(1)}, u32[]{:S(2)}, u32[]{:S(2)}) %collective-permute-start.3) | collective-permute-done | bytes 24608 | tf_op jit(solution)/shard_map/ppermute | solution.py:32
  10.4 3.1 %collective-permute-start.4 = (f32[3,8,128]{2,1,0:T(8,128)S(1)}, f32[3,8,128]{2,1,0:T(8,128)S(1)}, u32[]{:S(2)}, u32[]{:S(2)}) collective-permute-start(f32[3,8,128]{2,1,0:T(8,128)S(1)} %get-tuple-element.17), channel_id=1, source_target_pairs={{0,4},{1,5},{2,6},{3,7},{4,0},{5,1},{6,2},{7,3},{8,12},{9,13},{10,... | collective-permute-start | bytes 36872 | tf_op jit(solution)/shard_map/ppermute | solution.py:32
  13.5 2.1 %solve.1 = (f32[33,2,8,128]{3,2,1,0:T(8,128)S(1)}, f32[2,32,8,128]{3,2,1,0:T(8,128)S(1)}) custom-call(f32[8,8]{1,0:T(8,128)} %coupling_ref.1, f32[8,32,256]{2,1,0:T(8,128)S(1)} %get-tuple-element.11.state_ref, f32[1,32]{1,0:T(1,128)} %bitcast.108, f32[8,32,32]{2,1,0:T(8,128)S(1)} %get-tuple-element.12.inverse_ref), custom_call_target="tpu_custom_call" | custom-call | tf_op jit(solution)/shard_map/solve/pallas_call | solution.py:361
  15.6 0.1 collective-permute-start
  15.7 0.0 collective-permute-done.4
  15.7 1.5 %collective-permute-done.came_ref = f32[33,2,8,128]{3,2,1,0:T(8,128)S(1)} collective-permute-done((f32[33,2,8,128]{3,2,1,0:T(8,128)S(1)}, f32[33,2,8,128]{3,2,1,0:T(8,128)S(1)}, u32[]{:S(2)}, u32[]{:S(2)}) %collective-permute-start) | collective-permute-done | bytes 270368 | tf_op jit(solution)/shard_map/ppermute | solution.py:32
  17.2 0.8 %select.1.kept_ref = f32[33,2,8,128]{3,2,1,0:T(8,128)S(1)} custom-call(s32[32]{0:T(128)} %shifts_ref.5, f32[33,2,8,128]{3,2,1,0:T(8,128)S(1)} %get-tuple-element.14.kept_ref, f32[33,2,8,128]{3,2,1,0:T(8,128)S(1)} %collective-permute-done.came_ref), custom_call_target="tpu_custom_call" | custom-call | tf_op jit(solution)/shard_map/select/pallas_call | solution.py:379
  18.0 1.6 %collective-permute-start.1 = (f32[33,2,8,128]{3,2,1,0:T(8,128)S(1)}, f32[33,2,8,128]{3,2,1,0:T(8,128)S(1)}, u32[]{:S(2)}, u32[]{:S(2)}) collective-permute-start(f32[33,2,8,128]{3,2,1,0:T(8,128)S(1)} %select.1.kept_ref), channel_id=1, source_target_pairs={{0,16},{8,24},{16,0},{24,8},{1,17},{9,25},{17,1},{25,9},{2,18},{10... | collective-permute-start | bytes 811016 | tf_op jit(solution)/shard_map/ppermute | solution.py:32
  19.5 0.0 collective-permute-start.5
  19.6 1.2 %collective-permute-done.5.rest_1_ = f32[1,2,3,8,128]{4,3,2,1,0:T(8,128)S(1)} collective-permute-done((f32[1,2,3,8,128]{4,3,2,1,0:T(8,128)S(1)}, f32[1,2,3,8,128]{4,3,2,1,0:T(8,128)S(1)}, u32[]{:S(2)}, u32[]{:S(2)}) %collective-permute-start.5) | collective-permute-done | bytes 24608 | tf_op jit(solution)/shard_map/ppermute | solution.py:32
  20.8 0.5 %collective-permute-start.6 = (f32[2,2,3,8,128]{4,3,2,1,0:T(8,128)S(1)}, f32[2,2,3,8,128]{4,3,2,1,0:T(8,128)S(1)}, u32[]{:S(2)}, u32[]{:S(2)}) collective-permute-start(f32[2,2,3,8,128]{4,3,2,1,0:T(8,128)S(1)} %pad_maximum_fusion), channel_id=1, source_target_pairs={{0,16},{8,24},{16,0},{24,8},{1,17},{9,25},{17,1},{25,9},{2,18},{10... | collective-permute-start | bytes 147464 | tf_op jit(solution)/shard_map/ppermute | solution.py:32
  21.3 5.8 %collective-permute-done.1.came_ref = f32[33,2,8,128]{3,2,1,0:T(8,128)S(1)} collective-permute-done((f32[33,2,8,128]{3,2,1,0:T(8,128)S(1)}, f32[33,2,8,128]{3,2,1,0:T(8,128)S(1)}, u32[]{:S(2)}, u32[]{:S(2)}) %collective-permute-start.1) | collective-permute-done | bytes 270368 | tf_op jit(solution)/shard_map/ppermute | solution.py:32
  27.1 1.1 %rotate.1.rotated_ref = f32[32,2,8,128]{3,2,1,0:T(8,128)S(1)} custom-call(s32[32]{0:T(128)} %shifts_ref.5, f32[33,2,8,128]{3,2,1,0:T(8,128)S(1)} %select.1.kept_ref, f32[33,2,8,128]{3,2,1,0:T(8,128)S(1)} %collective-permute-done.1.came_ref), custom_call_target="tpu_custom_call" | custom-call | tf_op jit(solution)/shard_map/rotate/pallas_call | solution.py:387
  28.2 0.0 collective-permute-done.6.rest_2_
  28.2 1.7 %finish.1 = f32[8,32,256]{2,1,0:T(8,128)} custom-call(s32[32]{0:T(128)} %shifts_ref.5, f32[2,32,8,128]{3,2,1,0:T(8,128)S(1)} %get-tuple-element.13.columns_ref, f32[32,2,8,128]{3,2,1,0:T(8,128)S(1)} %rotate.1.rotated_ref, f32[1,2,3,8,128]{4,3,2,1,0:T(8,128)S(1)} %maximum_bitcast_fusion.rest_0_, f32[1,2,3,8,128]{4,3,2,1,0:T(8,128)S(1)} %collective-permute-done.5.rest_1_, ...), custom_call_target="tpu_custom_call" | custom-call | tf_op jit(solution)/shard_map/finish/pallas_call | solution.py:401
  (9 shorter events, 0.1 us)
Async XLA Ops:
  1.5 4.8 %collective-permute-start.2 = (f32[2,3,8,128]{3,2,1,0:T(8,128)S(1)}, f32[2,3,8,128]{3,2,1,0:T(8,128)S(1)}, u32[]{:S(2)}, u32[]{:S(2)}) collective-permute-start(f32[2,3,8,128]{3,2,1,0:T(8,128)S(1)} %get-tuple-element.16), channel_id=1, source_target_pairs={{0,1},{1,0},{2,3},{3,2},{4,5},{5,4},{6,7},{7,6},{8,9},{9,8},{10,11... | collective-permute-start | bytes 73736 | tf_op jit(solution)/shard_map/ppermute | solution.py:32
  6.4 4.0 %collective-permute-start.3 = (f32[2,3,8,128]{3,2,1,0:T(8,128)S(1)}, f32[2,3,8,128]{3,2,1,0:T(8,128)S(1)}, u32[]{:S(2)}, u32[]{:S(2)}) collective-permute-start(f32[2,3,8,128]{3,2,1,0:T(8,128)S(1)} %pad_maximum_fusion.1), channel_id=1, source_target_pairs={{0,2},{1,3},{2,0},{3,1},{4,6},{5,7},{6,4},{7,5},{8,10},{9,11},{10,... | collective-permute-start | bytes 73736 | tf_op jit(solution)/shard_map/ppermute | solution.py:32
  10.4 5.3 %collective-permute-start.4 = (f32[3,8,128]{2,1,0:T(8,128)S(1)}, f32[3,8,128]{2,1,0:T(8,128)S(1)}, u32[]{:S(2)}, u32[]{:S(2)}) collective-permute-start(f32[3,8,128]{2,1,0:T(8,128)S(1)} %get-tuple-element.17), channel_id=1, source_target_pairs={{0,4},{1,5},{2,6},{3,7},{4,0},{5,1},{6,2},{7,3},{8,12},{9,13},{10,... | collective-permute-start | bytes 36872 | tf_op jit(solution)/shard_map/ppermute | solution.py:32
  15.6 1.6 %collective-permute-start = (f32[33,2,8,128]{3,2,1,0:T(8,128)S(1)}, f32[33,2,8,128]{3,2,1,0:T(8,128)S(1)}, u32[]{:S(2)}, u32[]{:S(2)}) collective-permute-start(f32[33,2,8,128]{3,2,1,0:T(8,128)S(1)} %get-tuple-element.14.kept_ref), channel_id=1, source_target_pairs={{0,8},{8,0},{16,24},{24,16},{1,9},{9,1},{17,25},{25,17},{2,10},{10... | collective-permute-start | bytes 811016 | tf_op jit(solution)/shard_map/ppermute | solution.py:32
  18.0 9.1 %collective-permute-start.1 = (f32[33,2,8,128]{3,2,1,0:T(8,128)S(1)}, f32[33,2,8,128]{3,2,1,0:T(8,128)S(1)}, u32[]{:S(2)}, u32[]{:S(2)}) collective-permute-start(f32[33,2,8,128]{3,2,1,0:T(8,128)S(1)} %select.1.kept_ref), channel_id=1, source_target_pairs={{0,16},{8,24},{16,0},{24,8},{1,17},{9,25},{17,1},{25,9},{2,18},{10... | collective-permute-start | bytes 811016 | tf_op jit(solution)/shard_map/ppermute | solution.py:32
  19.5 1.2 %collective-permute-start.5 = (f32[1,2,3,8,128]{4,3,2,1,0:T(8,128)S(1)}, f32[1,2,3,8,128]{4,3,2,1,0:T(8,128)S(1)}, u32[]{:S(2)}, u32[]{:S(2)}) collective-permute-start(f32[1,2,3,8,128]{4,3,2,1,0:T(8,128)S(1)} %maximum_bitcast_fusion.rest_0_), channel_id=1, source_target_pairs={{0,8},{8,0},{16,24},{24,16},{1,9},{9,1},{17,25},{25,17},{2,10},{10... | collective-permute-start | bytes 73736 | tf_op jit(solution)/shard_map/ppermute | solution.py:32
  20.8 7.4 %collective-permute-start.6 = (f32[2,2,3,8,128]{4,3,2,1,0:T(8,128)S(1)}, f32[2,2,3,8,128]{4,3,2,1,0:T(8,128)S(1)}, u32[]{:S(2)}, u32[]{:S(2)}) collective-permute-start(f32[2,2,3,8,128]{4,3,2,1,0:T(8,128)S(1)} %pad_maximum_fusion), channel_id=1, source_target_pairs={{0,16},{8,24},{16,0},{24,8},{1,17},{9,25},{17,1},{25,9},{2,18},{10... | collective-permute-start | bytes 147464 | tf_op jit(solution)/shard_map/ppermute | solution.py:32

commit v3 on v2

--- a/solution.py
+++ b/solution.py
@@ -13,6 +13,10 @@
 SMEM = pl.BlockSpec(memory_space=pltpu.SMEM)
 VMEM = pl.BlockSpec(memory_space=pltpu.VMEM)
 ANY = pl.BlockSpec(memory_space=pl.ANY)
+
+
+def cost(kilobytes):
+    return pl.CostEstimate(flops=kilobytes << 18, bytes_accessed=kilobytes << 10, transcendentals=0)
 
 
 def in_vmem(x):
@@ -80,8 +84,8 @@
 
 
 def offsets_kernel(
-    count, state_hbm, inverse_hbm, velocity_hbm, coupling_hbm, diffusivity_hbm,
-    out_ref, coeffs_ref, state_ref, inverse_ref, velocity_ref, coupling_ref, diffusivity_ref, sems,
+    state_hbm, inverse_hbm, velocity_hbm, coupling_hbm, diffusivity_hbm,
+    out_ref, state_ref, inverse_ref, velocity_ref, coupling_ref, diffusivity_ref, sems,
 ):
     copies = [
         pltpu.make_async_copy(source, target, sems.at[i])
@@ -104,8 +108,6 @@
     diffusivity = as_column(diffusivity_ref[...])
     first = diffusivity * inverse_ref[:, 0, :]
     last = diffusivity * inverse_ref[:, rows - 1, :]
-    for i, x in enumerate(level_coefficients(first, last, count, lax.axis_index("rad"))):
-        coeffs_ref[i] = x
     first = jnp.concatenate([first] * fields, axis=1)
     last = jnp.concatenate([last] * fields, axis=1)
     speed = jnp.concatenate([jnp.broadcast_to(velocity_ref[...], (fields, rows))] * fields, axis=1)
@@ -142,14 +144,22 @@
 
 
 def solve_kernel(
-    count, coupling_ref, state_ref, velocity_ref, inverse_ref,
-    out_ref, columns_ref, diff_ref, updated_ref, table_ref,
+    count, segments, coupling_ref, state_ref, velocity_ref, diffusivity_ref, inverse_ref,
+    out_ref, columns_ref, coeffs_ref, final_ref, diff_ref, updated_ref, table_ref,
 ):
     fields, rows, cells = state_ref.shape
     span = fields * rows
     width = cells + LANES
     row = iota((rows, cells), 0)
     half = 0.5 * as_column(velocity_ref[...])
+    diffusivity = as_column(diffusivity_ref[...])
+    first = diffusivity * inverse_ref[:, 0, :]
+    last = diffusivity * inverse_ref[:, rows - 1, :]
+    for i, x in enumerate(level_coefficients(first, last, segments, lax.axis_index("rad"))):
+        if i < coeffs_ref.shape[0]:
+            coeffs_ref[i] = x
+        else:
+            final_ref[i - coeffs_ref.shape[0]] = x
     for g in range(fields):
         block = state_ref[g]
         upper = jnp.where(row == rows - 1, 0.0, pltpu.roll(block, rows - 1, 0))
@@ -197,15 +207,16 @@
 
 
 def masks(shift, cells, place, bit):
+    residue = shift & (cells - 1)
     hops = shift >> log2(cells)
-    residue = shift & (cells - 1)
     near = ((place - hops) ^ place) & bit
     far = ((place - hops - 1) ^ place) & bit
     lane = iota((8, LANES), 1)
     return [jnp.where(lane + j * LANES < cells - residue, near, far) != 0 for j in range(2)]
 
 
-def select_kernel(bit, shifts_ref, kept_ref, came_ref, out_ref):
+def select_kernel(bit, shifts_ref, kept_ref, came_ref, coeffs_ref, out_ref, later_ref):
+    later_ref[...] = coeffs_ref[...]
     rows = shifts_ref.shape[0]
     place = lax.axis_index("az")
     for r in range(rows):
@@ -300,36 +311,61 @@
         copy.wait()
 
 
-def chain(offsets, coeffs):
+def merge_kernel(level, count, first, *refs):
+    refs = list(refs)
+    own_ref, other_ref, coeffs_ref = refs[:3]
+    sums_ref = None if first else refs[3]
+    held_ref, sum_ref = refs[-2:] if not first else refs[5:7]
     place = lax.axis_index("rad")
-    count = lax.axis_size("rad")
-    head, tail = offsets[0], offsets[1]
-    left = right = None
-    bit = 1
-    at = 0
-    while 2 * bit < count:
-        upper = (place & bit) != 0
-        q, own, other_scale, felt_l, felt_r, b, c = [coeffs[at + i] for i in range(7)]
-        at += 7
-        other = swapped(jnp.stack([head, tail]), "rad", bit)
-        meeting = jnp.where(upper, other[1], other[0])
+    upper = iota((own_ref.shape[-2], LANES), 0) * 0 + (place & (1 << level)) != 0
+    following = iota((own_ref.shape[-2], LANES), 0) * 0 + (place & (2 << level)) != 0
+    q, own, other_scale, felt_l, felt_r, b, c = [coeffs_ref[7 * level + i] for i in range(7)]
+    for t in range(own_ref.shape[1]):
+        head, tail = own_ref[0, t], own_ref[1, t]
+        meeting = jnp.where(upper, other_ref[1, t], other_ref[0, t])
         facing = jnp.where(upper, head, tail)
         inner = q * meeting + own * facing
         partner = q * facing + other_scale * meeting
-        left = felt_l * inner if left is None else left + felt_l * inner
-        right = felt_r * inner if right is None else right + felt_r * inner
-        head = jnp.where(upper, other[0], head) + c * jnp.where(upper, partner, inner)
-        tail = jnp.where(upper, tail, other[1]) + b * jnp.where(upper, inner, partner)
-        bit *= 2
-    upper = (place & bit) != 0
-    facing = jnp.where(upper, head, tail)
-    meeting = swapped(facing, "rad", bit)
-    return jnp.stack(
-        [
-            left + coeffs[at] * meeting + coeffs[at + 1] * facing,
-            right + coeffs[at + 2] * meeting + coeffs[at + 3] * facing,
-        ]
-    )
+        if first:
+            sum_ref[0, t] = felt_l * inner
+            sum_ref[1, t] = felt_r * inner
+        else:
+            sum_ref[0, t] = sums_ref[0, t] + felt_l * inner
+            sum_ref[1, t] = sums_ref[1, t] + felt_r * inner
+        head = jnp.where(upper, other_ref[0, t], head) + c * jnp.where(upper, partner, inner)
+        tail = jnp.where(upper, tail, other_ref[1, t]) + b * jnp.where(upper, inner, partner)
+        if 4 << level == count:
+            held_ref[t] = jnp.where(following, head, tail)
+        else:
+            held_ref[0, t] = head
+            held_ref[1, t] = tail
+
+
+def merge(level, held, coeffs, extra):
+    count = lax.axis_size("rad")
+    first = level == 0
+    last = 4 << level == count
+    sums = pltpu.VMEM(held.shape, f32)
+    message = pltpu.VMEM(held.shape[1:] if last else held.shape, f32)
+    return pl.pallas_call(
+        functools.partial(merge_kernel, level, count, first),
+        out_shape=[pltpu.VMEM(extra.shape, f32), message, sums] if first else [message, sums],
+        in_specs=[VMEM] * 4,
+        out_specs=[VMEM] * (3 if first else 2),
+        input_output_aliases={3: 0} if first else {},
+        cost_estimate=cost(40000),
+        name="merge",
+    )(*map(in_vmem, (held, swapped(held, "rad", 1 << level), coeffs, extra)))
+
+
+def join_kernel(own_ref, other_ref, coeffs_ref, sums_ref, out_ref):
+    for e in range(2):
+        for t in range(own_ref.shape[0]):
+            out_ref[0, e, t] = (
+                sums_ref[e, t]
+                + coeffs_ref[2 * e] * other_ref[t]
+                + coeffs_ref[2 * e + 1] * own_ref[t]
+            )
 
 
 def per_device(state, velocity, coupling, diffusivity, inverse, shifts):
@@ -338,51 +374,55 @@
     tiles = cells // LANES
     assert tiles == 2 and fields == 8 and 2 * rows <= LANES
     count = lax.axis_size("az")
-    levels = log2(lax.axis_size("rad"))
-    offsets, coeffs, state_near, inverse_near = pl.pallas_call(
-        functools.partial(offsets_kernel, lax.axis_size("rad")),
+    segments = lax.axis_size("rad")
+    offsets, state_near, inverse_near = pl.pallas_call(
+        offsets_kernel,
         out_shape=[
             pltpu.VMEM((2, tiles + 1, fields, LANES), f32),
-            pltpu.VMEM((7 * levels - 3, fields, LANES), f32),
             pltpu.VMEM(state.shape, f32),
             pltpu.VMEM(inverse.shape, f32),
         ],
         in_specs=[ANY] * 5,
-        out_specs=[VMEM] * 4,
+        out_specs=[VMEM] * 3,
         scratch_shapes=[
             pltpu.VMEM((1, rows), f32),
             pltpu.VMEM((fields, fields), f32),
             pltpu.VMEM((1, fields), f32),
             pltpu.SemaphoreType.DMA((5,)),
         ],
+        cost_estimate=cost(5000),
         name="offsets",
     )(state, inverse, velocity[None], coupling, diffusivity[None])
     spare = count * 2 * rows // cells
-    solved, columns = pl.pallas_call(
-        functools.partial(solve_kernel, count),
+    solved, columns, coeffs, final = pl.pallas_call(
+        functools.partial(solve_kernel, count, segments),
         out_shape=[
             pltpu.VMEM((rows + spare, tiles, fields, LANES), f32),
             pltpu.VMEM((2, rows, fields, LANES), f32),
+            pltpu.VMEM((7 * log2(segments) - 7, fields, LANES), f32),
+            pltpu.VMEM((4, fields, LANES), f32),
         ],
-        in_specs=[SMEM] + [VMEM] * 3,
-        out_specs=[VMEM] * 2,
+        in_specs=[SMEM] + [VMEM] * 4,
+        out_specs=[VMEM] * 4,
         scratch_shapes=[
             pltpu.VMEM((fields, rows, cells), f32),
             pltpu.VMEM((fields * rows, cells + LANES), f32),
             pltpu.VMEM((fields * rows // LANES, fields * rows, LANES), f32),
         ],
+        cost_estimate=cost(8000),
         name="solve",
-    )(coupling, in_vmem(state_near), velocity[None], in_vmem(inverse_near))
-    kept = solved
+    )(coupling, in_vmem(state_near), velocity[None], diffusivity[None], in_vmem(inverse_near))
+    kept, held, sums = merge(0, offsets, coeffs, solved)
     bit = 1
     while 2 * bit < count:
-        kept = pl.pallas_call(
+        kept, coeffs = pl.pallas_call(
             functools.partial(select_kernel, bit),
-            out_shape=pltpu.VMEM(solved.shape, f32),
-            in_specs=[SMEM] + [VMEM] * 2,
-            out_specs=VMEM,
-            name="select",
-        )(shifts, in_vmem(kept), in_vmem(swapped(kept, "az", bit)))
+            out_shape=[pltpu.VMEM(kept.shape, f32), pltpu.VMEM(coeffs.shape, f32)],
+            in_specs=[SMEM] + [VMEM] * 3,
+            out_specs=[VMEM] * 2,
+            cost_estimate=cost(2800),
+        name="select",
+        )(shifts, in_vmem(kept), in_vmem(swapped(kept, "az", bit)), in_vmem(coeffs))
         bit *= 2
     rotated = pl.pallas_call(
         functools.partial(rotate_kernel, count, bit),
@@ -390,10 +430,20 @@
         in_specs=[SMEM] + [VMEM] * 2,
         out_specs=VMEM,
         scratch_shapes=[pltpu.VMEM((count * 2 * rows // LANES, fields, LANES), f32)],
+        cost_estimate=cost(4000),
         name="rotate",
     )(shifts, in_vmem(kept), in_vmem(swapped(kept, "az", bit)))
-    forcing = chain(offsets, coeffs)
-    parts = [forcing[None]]
+    for level in range(1, log2(segments) - 1):
+        held, sums = merge(level, held, coeffs, sums)
+    forcing = pl.pallas_call(
+        join_kernel,
+        out_shape=pltpu.VMEM((1,) + sums.shape, f32),
+        in_specs=[VMEM] * 4,
+        out_specs=VMEM,
+        cost_estimate=cost(400),
+        name="join",
+    )(*map(in_vmem, (held, swapped(held, "rad", segments // 2), final, sums)))
+    parts = [forcing]
     bit = 1
     while bit < count:
         parts.append(swapped(jnp.concatenate(parts, 0), "az", bit))
@@ -408,6 +458,7 @@
             pltpu.VMEM((rows // 8, tiles, 8 * fields, LANES), f32),
             pltpu.SemaphoreType.DMA((rows // 8, tiles)),
         ],
+        cost_estimate=cost(6000),
         name="finish",
     )(shifts, in_vmem(columns), in_vmem(rotated), *map(in_vmem, parts))
     return out[:, None]

time: 30.1 us -> 22.9 us (0.76)
  waiting for transfers between devices: 12.1 us -> 4.76 us
    ppermute x7, waiting for transfers between devices: 12.1 us -> 4.76 us  [swapped(): lax.ppermute(block, axis, [(i, i ^ bit) for i in range(lax.axis_size(axis...]
    pallas_call x3 -> x6, Pallas kernels: 4.38 us -> 4.47 us  [the longest x1 2.16 us: per_device(): pl.pallas_call(functools.partial(solve_kernel, count, segments), out_shap...]
  transfers between devices with their start and end apart: 7 -> 7, of which waited for: 5 -> 3; matrix products, arithmetic and copies ran while one was open for 0% -> 0% of each run, Pallas kernels for 11% -> 18%
where the time goes in v3:
time: 22.9 us; the launch traced here: 22.7 us
  starting transfers between devices  10.6 us (46%)
  Pallas kernels  7.29 us (32%)
  waiting for transfers between devices  4.76 us (21%)
    ppermute x7, starting transfers between devices, swapped(): lax.ppermute(block, axis, [(i, i ^ bit) for i in range(lax.axis_size(axis...  10.6 us
    ppermute x7, waiting for transfers between devices, swapped(): lax.ppermute(block, axis, [(i, i ^ bit) for i in range(lax.axis_size(axis...  4.76 us
    pallas_call x1, Pallas kernels, per_device(): pl.pallas_call(functools.partial(solve_kernel, count, segments), out_shap...  2.16 us
    pallas_call x1, Pallas kernels, per_device(): pl.pallas_call(functools.partial(finish_kernel, count, len(parts)), out_s...  1.71 us
    pallas_call x1, Pallas kernels, per_device(): pl.pallas_call(offsets_kernel, out_shape=[pltpu.VMEM((2, tiles + 1, field...  1.5 us
    pallas_call x1, Pallas kernels, per_device(): pl.pallas_call(functools.partial(rotate_kernel, count, bit), out_shape=pl...  1.11 us
    pallas_call x1, Pallas kernels, per_device(): pl.pallas_call(functools.partial(select_kernel, bit), out_shape=[pltpu.VM...  0.76 us
  transfers between devices with their start and end apart: 7, of which 3 were waited for; matrix products, arithmetic and copies ran while one was open for 0% of the time, Pallas kernels for 18%

profile of v3, /device:TPU:0, one launch (start us, length us, event | category | flops | bytes accessed | tf_op | source)
XLA Modules:
  0.0 22.7 jit_solution(11913375966478723473)
XLA Ops:
  0.0 1.5 %offsets.1 = (f32[2,3,8,128]{3,2,1,0:T(8,128)S(1)}, f32[8,32,256]{2,1,0:T(8,128)S(1)}, f32[8,32,32]{2,1,0:T(8,128)S(1)}) custom-call(f32[8,32,256]{2,1,0:T(8,128)} %bitcast.6, f32[8,32,32]{2,1,0:T(8,128)} %inverse_hbm.1, f32[1,32]{1,0:T(1,128)} %bitcast.7, f32[8,8]{1,0:T(8,128)} %coupling_ref.1, f32[1,8]{1,0:T(1,128)} %bitcast.9), custom_call_target="tpu_custom_call" | custom-call | flops 1310720000 | bytes 5120000 | tf_op jit(solution)/shard_map/offsets/pallas_call | solution.py:378
  1.5 3.0 %collective-permute-start = (f32[2,3,8,128]{3,2,1,0:T(8,128)S(1)}, f32[2,3,8,128]{3,2,1,0:T(8,128)S(1)}, u32[]{:S(2)}, u32[]{:S(2)}) collective-permute-start(f32[2,3,8,128]{3,2,1,0:T(8,128)S(1)} %get-tuple-element.22.refs_0_), channel_id=1, source_target_pairs={{0,1},{1,0},{2,3},{3,2},{4,5},{5,4},{6,7},{7,6},{8,9},{9,8},{10,11... | collective-permute-start | bytes 73736 | tf_op jit(solution)/shard_map/ppermute | solution.py:36
  4.5 2.2 %solve.1 = (f32[33,2,8,128]{3,2,1,0:T(8,128)S(1)}, f32[2,32,8,128]{3,2,1,0:T(8,128)S(1)}, f32[14,8,128]{2,1,0:T(8,128)S(1)}, f32[4,8,128]{2,1,0:T(8,128)S(1)}) custom-call(f32[8,8]{1,0:T(8,128)} %coupling_ref.1, f32[8,32,256]{2,1,0:T(8,128)S(1)} %get-tuple-element.19.state_ref, f32[1,32]{1,0:T(1,128)} %bitcast.8, f32[1,8]{1,0:T(1,128)} %bitcast.10, ...), custom_call_target="tpu_custom_call" | custom-call | flops 2097152000 | bytes 8192000 | tf_op jit(solution)/shard_map/solve/pallas_call | solution.py:397
  6.7 0.0 collective-permute-done.refs_1_
  6.7 0.1 collective-permute-start.1
  6.8 1.8 %collective-permute-start.3 = (f32[2,3,8,128]{3,2,1,0:T(8,128)S(1)}, f32[2,3,8,128]{3,2,1,0:T(8,128)S(1)}, u32[]{:S(2)}, u32[]{:S(2)}) collective-permute-start(f32[2,3,8,128]{3,2,1,0:T(8,128)S(1)} %get-tuple-element.27.refs_0_), channel_id=1, source_target_pairs={{0,2},{1,3},{2,0},{3,1},{4,6},{5,7},{6,4},{7,5},{8,10},{9,11},{10,... | collective-permute-start | bytes 73736 | tf_op jit(solution)/shard_map/ppermute | solution.py:36
  8.6 0.0 collective-permute-done.1.came_ref
  8.6 0.8 %select.1 = (f32[33,2,8,128]{3,2,1,0:T(8,128)S(1)}, f32[14,8,128]{2,1,0:T(8,128)S(1)}) custom-call(s32[32]{0:T(128)} %shifts_ref.5, f32[33,2,8,128]{3,2,1,0:T(8,128)S(1)} %get-tuple-element.25.kept_ref, f32[33,2,8,128]{3,2,1,0:T(8,128)S(1)} %collective-permute-done.1.came_ref, f32[14,8,128]{2,1,0:T(8,128)S(1)} %get-tuple-element.23.refs_2_.coeffs_ref), custom_call_target="tpu_custom_call" | custom-call | flops 734003200 | bytes 2867200 | tf_op jit(solution)/shard_map/select/pallas_call | solution.py:418
  9.4 1.6 %collective-permute-start.2 = (f32[33,2,8,128]{3,2,1,0:T(8,128)S(1)}, f32[33,2,8,128]{3,2,1,0:T(8,128)S(1)}, u32[]{:S(2)}, u32[]{:S(2)}) collective-permute-start(f32[33,2,8,128]{3,2,1,0:T(8,128)S(1)} %get-tuple-element.26.kept_ref), channel_id=1, source_target_pairs={{0,16},{8,24},{16,0},{24,8},{1,17},{9,25},{17,1},{25,9},{2,18},{10... | collective-permute-start | bytes 811016 | tf_op jit(solution)/shard_map/ppermute | solution.py:36
  10.9 0.0 collective-permute-done.3.refs_1_
  11.0 2.7 %collective-permute-start.4 = (f32[3,8,128]{2,1,0:T(8,128)S(1)}, f32[3,8,128]{2,1,0:T(8,128)S(1)}, u32[]{:S(2)}, u32[]{:S(2)}) collective-permute-start(f32[3,8,128]{2,1,0:T(8,128)S(1)} %get-tuple-element.30.own_ref), channel_id=1, source_target_pairs={{0,4},{1,5},{2,6},{3,7},{4,0},{5,1},{6,2},{7,3},{8,12},{9,13},{10,... | collective-permute-start | bytes 36872 | tf_op jit(solution)/shard_map/ppermute | solution.py:36
  13.6 2.0 %collective-permute-done.4.other_ref = f32[3,8,128]{2,1,0:T(8,128)S(1)} collective-permute-done((f32[3,8,128]{2,1,0:T(8,128)S(1)}, f32[3,8,128]{2,1,0:T(8,128)S(1)}, u32[]{:S(2)}, u32[]{:S(2)}) %collective-permute-start.4) | collective-permute-done | bytes 12320 | tf_op jit(solution)/shard_map/ppermute | solution.py:36
  15.6 0.1 collective-permute-start.5
  15.7 1.2 %collective-permute-done.5.rest_1_ = f32[1,2,3,8,128]{4,3,2,1,0:T(8,128)S(1)} collective-permute-done((f32[1,2,3,8,128]{4,3,2,1,0:T(8,128)S(1)}, f32[1,2,3,8,128]{4,3,2,1,0:T(8,128)S(1)}, u32[]{:S(2)}, u32[]{:S(2)}) %collective-permute-start.5) | collective-permute-done | bytes 24608 | tf_op jit(solution)/shard_map/ppermute | solution.py:36
  16.9 1.4 %collective-permute-start.6 = (f32[2,2,3,8,128]{4,3,2,1,0:T(8,128)S(1)}, f32[2,2,3,8,128]{4,3,2,1,0:T(8,128)S(1)}, u32[]{:S(2)}, u32[]{:S(2)}) collective-permute-start(f32[2,2,3,8,128]{4,3,2,1,0:T(8,128)S(1)} %pad_maximum_fusion), channel_id=1, source_target_pairs={{0,16},{8,24},{16,0},{24,8},{1,17},{9,25},{17,1},{25,9},{2,18},{10... | collective-permute-start | bytes 147464 | tf_op jit(solution)/shard_map/ppermute | solution.py:36
  18.3 0.0 collective-permute-done.2.came_ref
  18.3 1.1 %rotate.1.rotated_ref = f32[32,2,8,128]{3,2,1,0:T(8,128)S(1)} custom-call(s32[32]{0:T(128)} %shifts_ref.5, f32[33,2,8,128]{3,2,1,0:T(8,128)S(1)} %get-tuple-element.26.kept_ref, f32[33,2,8,128]{3,2,1,0:T(8,128)S(1)} %collective-permute-done.2.came_ref), custom_call_target="tpu_custom_call" | custom-call | flops 1048576000 | bytes 4096000 | tf_op jit(solution)/shard_map/rotate/pallas_call | solution.py:427
  19.4 1.6 %collective-permute-done.6.rest_2_ = f32[2,2,3,8,128]{4,3,2,1,0:T(8,128)S(1)} collective-permute-done((f32[2,2,3,8,128]{4,3,2,1,0:T(8,128)S(1)}, f32[2,2,3,8,128]{4,3,2,1,0:T(8,128)S(1)}, u32[]{:S(2)}, u32[]{:S(2)}) %collective-permute-start.6) | collective-permute-done | bytes 49184 | tf_op jit(solution)/shard_map/ppermute | solution.py:36
  21.0 1.7 %finish.1 = f32[8,32,256]{2,1,0:T(8,128)} custom-call(s32[32]{0:T(128)} %shifts_ref.5, f32[2,32,8,128]{3,2,1,0:T(8,128)S(1)} %get-tuple-element.21.columns_ref, f32[32,2,8,128]{3,2,1,0:T(8,128)S(1)} %rotate.1.rotated_ref, f32[1,2,3,8,128]{4,3,2,1,0:T(8,128)S(1)} %join.1.rest_0_, f32[1,2,3,8,128]{4,3,2,1,0:T(8,128)S(1)} %collective-permute-done.5.rest_1_, ...), custom_call_target="tpu_custom_call" | custom-call | flops 1572864000 | bytes 6144000 | tf_op jit(solution)/shard_map/finish/pallas_call | solution.py:451
  (4 shorter events, 0.1 us)
Async XLA Ops:
  1.5 5.2 %collective-permute-start = (f32[2,3,8,128]{3,2,1,0:T(8,128)S(1)}, f32[2,3,8,128]{3,2,1,0:T(8,128)S(1)}, u32[]{:S(2)}, u32[]{:S(2)}) collective-permute-start(f32[2,3,8,128]{3,2,1,0:T(8,128)S(1)} %get-tuple-element.22.refs_0_), channel_id=1, source_target_pairs={{0,1},{1,0},{2,3},{3,2},{4,5},{5,4},{6,7},{7,6},{8,9},{9,8},{10,11... | collective-permute-start | bytes 73736 | tf_op jit(solution)/shard_map/ppermute | solution.py:36
  6.7 1.9 %collective-permute-start.1 = (f32[33,2,8,128]{3,2,1,0:T(8,128)S(1)}, f32[33,2,8,128]{3,2,1,0:T(8,128)S(1)}, u32[]{:S(2)}, u32[]{:S(2)}) collective-permute-start(f32[33,2,8,128]{3,2,1,0:T(8,128)S(1)} %get-tuple-element.25.kept_ref), channel_id=1, source_target_pairs={{0,8},{8,0},{16,24},{24,16},{1,9},{9,1},{17,25},{25,17},{2,10},{10... | collective-permute-start | bytes 811016 | tf_op jit(solution)/shard_map/ppermute | solution.py:36
  6.8 4.1 %collective-permute-start.3 = (f32[2,3,8,128]{3,2,1,0:T(8,128)S(1)}, f32[2,3,8,128]{3,2,1,0:T(8,128)S(1)}, u32[]{:S(2)}, u32[]{:S(2)}) collective-permute-start(f32[2,3,8,128]{3,2,1,0:T(8,128)S(1)} %get-tuple-element.27.refs_0_), channel_id=1, source_target_pairs={{0,2},{1,3},{2,0},{3,1},{4,6},{5,7},{6,4},{7,5},{8,10},{9,11},{10,... | collective-permute-start | bytes 73736 | tf_op jit(solution)/shard_map/ppermute | solution.py:36
  9.4 9.0 %collective-permute-start.2 = (f32[33,2,8,128]{3,2,1,0:T(8,128)S(1)}, f32[33,2,8,128]{3,2,1,0:T(8,128)S(1)}, u32[]{:S(2)}, u32[]{:S(2)}) collective-permute-start(f32[33,2,8,128]{3,2,1,0:T(8,128)S(1)} %get-tuple-element.26.kept_ref), channel_id=1, source_target_pairs={{0,16},{8,24},{16,0},{24,8},{1,17},{9,25},{17,1},{25,9},{2,18},{10... | collective-permute-start | bytes 811016 | tf_op jit(solution)/shard_map/ppermute | solution.py:36
  11.0 4.7 %collective-permute-start.4 = (f32[3,8,128]{2,1,0:T(8,128)S(1)}, f32[3,8,128]{2,1,0:T(8,128)S(1)}, u32[]{:S(2)}, u32[]{:S(2)}) collective-permute-start(f32[3,8,128]{2,1,0:T(8,128)S(1)} %get-tuple-element.30.own_ref), channel_id=1, source_target_pairs={{0,4},{1,5},{2,6},{3,7},{4,0},{5,1},{6,2},{7,3},{8,12},{9,13},{10,... | collective-permute-start | bytes 36872 | tf_op jit(solution)/shard_map/ppermute | solution.py:36
  15.6 1.3 %collective-permute-start.5 = (f32[1,2,3,8,128]{4,3,2,1,0:T(8,128)S(1)}, f32[1,2,3,8,128]{4,3,2,1,0:T(8,128)S(1)}, u32[]{:S(2)}, u32[]{:S(2)}) collective-permute-start(f32[1,2,3,8,128]{4,3,2,1,0:T(8,128)S(1)} %join.1.rest_0_), channel_id=1, source_target_pairs={{0,8},{8,0},{16,24},{24,16},{1,9},{9,1},{17,25},{25,17},{2,10},{10... | collective-permute-start | bytes 73736 | tf_op jit(solution)/shard_map/ppermute | solution.py:36
  16.9 4.1 %collective-permute-start.6 = (f32[2,2,3,8,128]{4,3,2,1,0:T(8,128)S(1)}, f32[2,2,3,8,128]{4,3,2,1,0:T(8,128)S(1)}, u32[]{:S(2)}, u32[]{:S(2)}) collective-permute-start(f32[2,2,3,8,128]{4,3,2,1,0:T(8,128)S(1)} %pad_maximum_fusion), channel_id=1, source_target_pairs={{0,16},{8,24},{16,0},{24,8},{1,17},{9,25},{17,1},{25,9},{2,18},{10... | collective-permute-start | bytes 147464 | tf_op jit(solution)/shard_map/ppermute | solution.py:36

commit v4 on v3

--- a/solution.py
+++ b/solution.py
@@ -10,6 +10,7 @@
 highest = lax.Precision.HIGHEST
 f32 = jnp.float32
 LANES = 128
+BATCH = 8
 SMEM = pl.BlockSpec(memory_space=pltpu.SMEM)
 VMEM = pl.BlockSpec(memory_space=pltpu.VMEM)
 ANY = pl.BlockSpec(memory_space=pl.ANY)
@@ -21,6 +22,10 @@
 
 def in_vmem(x):
     return pltpu.with_memory_space_constraint(x, pltpu.VMEM)
+
+
+def in_smem(x):
+    return pltpu.with_memory_space_constraint(x, pltpu.SMEM)
 
 
 def iota(shape, dim):
@@ -84,8 +89,9 @@
 
 
 def offsets_kernel(
-    state_hbm, inverse_hbm, velocity_hbm, coupling_hbm, diffusivity_hbm,
-    out_ref, state_ref, inverse_ref, velocity_ref, coupling_ref, diffusivity_ref, sems,
+    state_hbm, inverse_hbm, velocity_hbm, coupling_hbm, diffusivity_hbm, shifts_hbm,
+    out_ref, state_ref, inverse_ref, velocity_ref, diffusivity_ref, shifts_ref, mixing_ref,
+    coupling_ref, sems,
 ):
     copies = [
         pltpu.make_async_copy(source, target, sems.at[i])
@@ -96,6 +102,8 @@
                 (coupling_hbm, coupling_ref),
                 (diffusivity_hbm, diffusivity_ref),
                 (state_hbm, state_ref),
+                (shifts_hbm, shifts_ref),
+                (coupling_hbm, mixing_ref),
             )
         )
     ]
@@ -141,6 +149,8 @@
     for e in range(2):
         for j in range(width // LANES):
             out_ref[e, j] = tile(total[e * fields : (e + 1) * fields], j)
+    for copy in copies[5:]:
+        copy.wait()
 
 
 def solve_kernel(
@@ -219,10 +229,14 @@
     later_ref[...] = coeffs_ref[...]
     rows = shifts_ref.shape[0]
     place = lax.axis_index("az")
-    for r in range(rows):
-        take = masks(shifts_ref[r], 2 * LANES, place, bit)
-        for j in range(2):
-            out_ref[r, j] = jnp.where(take[j], came_ref[r, j], kept_ref[r, j])
+    for batch in range(0, rows, BATCH):
+        values = []
+        for r in range(batch, batch + BATCH):
+            take = masks(shifts_ref[r], 2 * LANES, place, bit)
+            values.append([jnp.where(take[j], came_ref[r, j], kept_ref[r, j]) for j in range(2)])
+        for r, value in zip(range(batch, batch + BATCH), values):
+            for j in range(2):
+                out_ref[r, j] = value[j]
     out_ref[rows:] = kept_ref[rows:] + came_ref[rows:]
 
 
@@ -241,32 +255,33 @@
     lane = iota((fields, lanes), 1)
     for at in range(count * 2 * rows // lanes):
         ghosts_ref[at] = kept_ref[rows + at // 2, at % 2] + came_ref[rows + at // 2, at % 2]
-    for r in range(rows):
-        shift = shifts_ref[r]
-        hops = shift >> log2(cells)
-        residue = shift & (cells - 1)
-        take = masks(shift, cells, place, bit)
-        value = [jnp.where(take[j], came_ref[r, j], kept_ref[r, j]) for j in range(2)]
-        here = (place - hops) & (count - 1)
-        before = (here - 1) & (count - 1)
-        after = jnp.where(residue > 0, here, (here + 1) & (count - 1))
-        low_at = (before & (per_tile - 1)) * 2 * rows + r
-        high_at = (after & (per_tile - 1)) * 2 * rows + rows + r
-        low = pltpu.roll(ghosts_ref[before >> log2(per_tile)], (lanes - low_at) & (lanes - 1), 1)
-        high = pltpu.roll(ghosts_ref[after >> log2(per_tile)], lanes - 1 - high_at, 1)
-        value[0] = value[0] + jnp.where(lane == 0, low, 0.0)
-        value[1] = value[1] + jnp.where(lane == lanes - 1, high, 0.0)
-        value = turned(value, residue)
-        swap = residue >> log2(lanes)
-        out_ref[r, swap] = value[0]
-        out_ref[r, 1 - swap] = value[1]
+    for batch in range(0, rows, BATCH):
+        values = []
+        for r in range(batch, batch + BATCH):
+            shift = shifts_ref[r]
+            hops = shift >> log2(cells)
+            residue = shift & (cells - 1)
+            take = masks(shift, cells, place, bit)
+            value = [jnp.where(take[j], came_ref[r, j], kept_ref[r, j]) for j in range(2)]
+            here = (place - hops) & (count - 1)
+            before = (here - 1) & (count - 1)
+            after = jnp.where(residue > 0, here, (here + 1) & (count - 1))
+            low_at = (before & (per_tile - 1)) * 2 * rows + r
+            high_at = (after & (per_tile - 1)) * 2 * rows + rows + r
+            low = pltpu.roll(ghosts_ref[before >> log2(per_tile)], (lanes - low_at) & (lanes - 1), 1)
+            high = pltpu.roll(ghosts_ref[after >> log2(per_tile)], lanes - 1 - high_at, 1)
+            value[0] = value[0] + jnp.where(lane == 0, low, 0.0)
+            value[1] = value[1] + jnp.where(lane == lanes - 1, high, 0.0)
+            values.append((r, residue >> log2(lanes), turned(value, residue)))
+        for r, swap, value in values:
+            out_ref[r, swap] = value[0]
+            out_ref[r, 1 - swap] = value[1]
 
 
 def finish_kernel(count, parts, shifts_ref, columns_ref, rotated_ref, *rest):
     out_hbm, forcing_ref, total_ref, sems = rest[parts:]
     rows, tiles, fields, lanes = rotated_ref.shape
     cells = tiles * lanes
-    chunk = 8
     at = 0
     place = lax.axis_index("az")
     lane = iota((fields, lanes), 1)
@@ -280,33 +295,39 @@
             forcing_ref[m, e, 0] += jnp.where(lane == 0, forcing_ref[before, e, tiles], 0.0)
             forcing_ref[m, e, 1] += jnp.where(lane == lanes - 1, forcing_ref[after, e, tiles], 0.0)
     copies = []
-    for r in range(rows):
-        shift = shifts_ref[r]
-        hops = shift >> log2(cells)
-        residue = shift & (cells - 1)
-        here = (place - hops) & (count - 1)
-        source = here ^ place
-        source_low = ((here - 1) & (count - 1)) ^ place
-        value = []
+    for batch in range(0, rows, BATCH):
+        values = []
+        for r in range(batch, batch + BATCH):
+            shift = shifts_ref[r]
+            hops = shift >> log2(cells)
+            residue = shift & (cells - 1)
+            here = (place - hops) & (count - 1)
+            source = here ^ place
+            source_low = ((here - 1) & (count - 1)) ^ place
+            value = []
+            for j in range(2):
+                near = lane + j * lanes < cells - residue
+                left = jnp.where(near, forcing_ref[source, 0, j], forcing_ref[source_low, 0, j])
+                right = jnp.where(near, forcing_ref[source, 1, j], forcing_ref[source_low, 1, j])
+                value.append(columns_ref[0, r] * left + columns_ref[1, r] * right)
+            value = turned(value, residue)
+            swap = residue >> log2(lanes)
+            values.append(
+                (swap, value[0] + rotated_ref[r, swap], value[1] + rotated_ref[r, 1 - swap])
+            )
+        at = batch // BATCH
+        for i, (swap, near, far) in enumerate(values):
+            total_ref[at, swap, pl.ds(i, fields, stride=BATCH), :] = near
+            total_ref[at, 1 - swap, pl.ds(i, fields, stride=BATCH), :] = far
         for j in range(2):
-            near = lane + j * lanes < cells - residue
-            left = jnp.where(near, forcing_ref[source, 0, j], forcing_ref[source_low, 0, j])
-            right = jnp.where(near, forcing_ref[source, 1, j], forcing_ref[source_low, 1, j])
-            value.append(columns_ref[0, r] * left + columns_ref[1, r] * right)
-        value = turned(value, residue)
-        swap = residue >> log2(lanes)
-        for j, x in ((swap, value[0]), (1 - swap, value[1])):
-            total_ref[r // chunk, j, pl.ds(r % chunk, fields, stride=chunk), :] = x + rotated_ref[r, j]
-        if r % chunk == chunk - 1:
-            for j in range(2):
-                copies.append(
-                    pltpu.make_async_copy(
-                        total_ref.at[r // chunk, j].reshape(fields, chunk, lanes),
-                        out_hbm.at[:, pl.ds(r + 1 - chunk, chunk), pl.ds(j * lanes, lanes)],
-                        sems.at[r // chunk, j],
-                    )
+            copies.append(
+                pltpu.make_async_copy(
+                    total_ref.at[at, j].reshape(fields, BATCH, lanes),
+                    out_hbm.at[:, pl.ds(batch, BATCH), pl.ds(j * lanes, lanes)],
+                    sems.at[at, j],
                 )
-                copies[-1].start()
+            )
+            copies[-1].start()
     for copy in copies:
         copy.wait()
 
@@ -375,24 +396,27 @@
     assert tiles == 2 and fields == 8 and 2 * rows <= LANES
     count = lax.axis_size("az")
     segments = lax.axis_size("rad")
-    offsets, state_near, inverse_near = pl.pallas_call(
+    offsets, state_near, inverse_near, velocity, diffusivity, shifts, mixing = pl.pallas_call(
         offsets_kernel,
         out_shape=[
             pltpu.VMEM((2, tiles + 1, fields, LANES), f32),
             pltpu.VMEM(state.shape, f32),
             pltpu.VMEM(inverse.shape, f32),
+            pltpu.VMEM((1, rows), f32),
+            pltpu.VMEM((1, fields), f32),
+            pltpu.SMEM(shifts.shape, jnp.int32),
+            pltpu.SMEM(coupling.shape, f32),
         ],
-        in_specs=[ANY] * 5,
-        out_specs=[VMEM] * 3,
+        in_specs=[ANY] * 6,
+        out_specs=[VMEM] * 5 + [SMEM] * 2,
         scratch_shapes=[
-            pltpu.VMEM((1, rows), f32),
             pltpu.VMEM((fields, fields), f32),
-            pltpu.VMEM((1, fields), f32),
-            pltpu.SemaphoreType.DMA((5,)),
+            pltpu.SemaphoreType.DMA((7,)),
         ],
         cost_estimate=cost(5000),
         name="offsets",
-    )(state, inverse, velocity[None], coupling, diffusivity[None])
+    )(state, inverse, velocity[None], coupling, diffusivity[None], shifts)
+    shifts = in_smem(shifts)
     spare = count * 2 * rows // cells
     solved, columns, coeffs, final = pl.pallas_call(
         functools.partial(solve_kernel, count, segments),
@@ -411,7 +435,7 @@
         ],
         cost_estimate=cost(8000),
         name="solve",
-    )(coupling, in_vmem(state_near), velocity[None], diffusivity[None], in_vmem(inverse_near))
+    )(in_smem(mixing), *map(in_vmem, (state_near, velocity, diffusivity, inverse_near)))
     kept, held, sums = merge(0, offsets, coeffs, solved)
     bit = 1
     while 2 * bit < count:
@@ -446,8 +470,9 @@
     parts = [forcing]
     bit = 1
     while bit < count:
-        parts.append(swapped(jnp.concatenate(parts, 0), "az", bit))
-        bit *= 2
+        ours = parts[0] if len(parts) == 1 else jnp.concatenate(parts, 0)
+        parts += [swapped(ours, "az", i * bit) for i in range(1, min(4, count // bit))]
+        bit *= 4
     out = pl.pallas_call(
         functools.partial(finish_kernel, count, len(parts)),
         out_shape=jax.ShapeDtypeStruct(state.shape, f32),
@@ -455,8 +480,8 @@
         out_specs=ANY,
         scratch_shapes=[
             pltpu.VMEM((count, 2, tiles + 1, fields, LANES), f32),
-            pltpu.VMEM((rows // 8, tiles, 8 * fields, LANES), f32),
-            pltpu.SemaphoreType.DMA((rows // 8, tiles)),
+            pltpu.VMEM((rows // BATCH, tiles, BATCH * fields, LANES), f32),
+            pltpu.SemaphoreType.DMA((rows // BATCH, tiles)),
         ],
         cost_estimate=cost(6000),
         name="finish",

time: 22.9 us -> 21.7 us (0.948)
  the two profiles are of different devices: /device:TPU:0 before, /device:TPU:1 now
where the time goes in v4:
time: 21.7 us; the launch traced here: 21.2 us
  starting transfers between devices  12.8 us (59%)
  Pallas kernels  4.61 us (21%)
  waiting for transfers between devices  3.82 us (18%)
    ppermute x8, starting transfers between devices, swapped(): lax.ppermute(block, axis, [(i, i ^ bit) for i in range(lax.axis_size(axis...  12.8 us
    ppermute x8, waiting for transfers between devices, swapped(): lax.ppermute(block, axis, [(i, i ^ bit) for i in range(lax.axis_size(axis...  3.82 us
    pallas_call x1, Pallas kernels, per_device(): pl.pallas_call(offsets_kernel, out_shape=[pltpu.VMEM((2, tiles + 1, field...  1.53 us
    pallas_call x1, Pallas kernels, per_device(): pl.pallas_call(functools.partial(solve_kernel, count, segments), out_shap...  1.44 us
    pallas_call x1, Pallas kernels, per_device(): pl.pallas_call(functools.partial(finish_kernel, count, len(parts)), out_s...  1.05 us
    pallas_call x1, Pallas kernels, per_device(): pl.pallas_call(functools.partial(rotate_kernel, count, bit), out_shape=pl...  0.44 us
  transfers between devices with their start and end apart: 8, of which 3 were waited for; matrix products, arithmetic and copies ran while one was open for 0% of the time, Pallas kernels for 9%

profile of v4, /device:TPU:1, one launch (start us, length us, event | category | flops | bytes accessed | tf_op | source)
XLA Modules:
  0.0 21.2 jit_solution(17096078665012809061)
XLA Ops:
  0.0 1.5 %offsets.1 = (f32[2,3,8,128]{3,2,1,0:T(8,128)S(1)}, f32[8,32,256]{2,1,0:T(8,128)S(1)}, f32[8,32,32]{2,1,0:T(8,128)S(1)}, f32[1,32]{1,0:T(1,128)S(1)}, f32[1,8]{1...) custom-call(f32[8,32,256]{2,1,0:T(8,128)} %bitcast.6, f32[8,32,32]{2,1,0:T(8,128)} %inverse_hbm.1, f32[1,32]{1,0:T(1,128)} %bitcast.7, ...), custom_call_target="tpu_custom_call" | custom-call | flops 1310720000 | bytes 5120000 | tf_op jit(solution)/shard_map/offsets/pallas_call | solution.py:399
  1.5 2.1 %collective-permute-start = (f32[2,3,8,128]{3,2,1,0:T(8,128)S(1)}, f32[2,3,8,128]{3,2,1,0:T(8,128)S(1)}, u32[]{:S(2)}, u32[]{:S(2)}) collective-permute-start(f32[2,3,8,128]{3,2,1,0:T(8,128)S(1)} %get-tuple-element.30.refs_0_), channel_id=1, source_target_pairs={{0,1},{1,0},{2,3},{3,2},{4,5},{5,4},{6,7},{7,6},{8,9},{9,8},{10,11... | collective-permute-start | bytes 73736 | tf_op jit(solution)/shard_map/ppermute | solution.py:41
  3.6 1.4 %solve.1 = (f32[33,2,8,128]{3,2,1,0:T(8,128)S(1)}, f32[2,32,8,128]{3,2,1,0:T(8,128)S(1)}, f32[14,8,128]{2,1,0:T(8,128)S(1)}, f32[4,8,128]{2,1,0:T(8,128)S(1)}) custom-call(f32[8,8]{1,0:T(8,128)S(4)} %get-tuple-element.24.coupling_ref, f32[8,32,256]{2,1,0:T(8,128)S(1)} %get-tuple-element.25.state_ref, f32[1,32]{1,0:T(1,128)S(1)} %get-tuple-element.26.velocity_ref, ...), custom_call_target="tpu_custom_call" | custom-call | flops 2097152000 | bytes 8192000 | tf_op jit(solution)/shard_map/solve/pallas_call | solution.py:421
  5.1 0.0 collective-permute-done.refs_1_
  5.1 1.4 %collective-permute-start.1 = (f32[33,2,8,128]{3,2,1,0:T(8,128)S(1)}, f32[33,2,8,128]{3,2,1,0:T(8,128)S(1)}, u32[]{:S(2)}, u32[]{:S(2)}) collective-permute-start(f32[33,2,8,128]{3,2,1,0:T(8,128)S(1)} %get-tuple-element.33.kept_ref), channel_id=1, source_target_pairs={{0,8},{8,0},{16,24},{24,16},{1,9},{9,1},{17,25},{25,17},{2,10},{10... | collective-permute-start | bytes 811016 | tf_op jit(solution)/shard_map/ppermute | solution.py:41
  6.5 1.8 %collective-permute-start.3 = (f32[2,3,8,128]{3,2,1,0:T(8,128)S(1)}, f32[2,3,8,128]{3,2,1,0:T(8,128)S(1)}, u32[]{:S(2)}, u32[]{:S(2)}) collective-permute-start(f32[2,3,8,128]{3,2,1,0:T(8,128)S(1)} %get-tuple-element.35.refs_0_), channel_id=1, source_target_pairs={{0,2},{1,3},{2,0},{3,1},{4,6},{5,7},{6,4},{7,5},{8,10},{9,11},{10,... | collective-permute-start | bytes 73736 | tf_op jit(solution)/shard_map/ppermute | solution.py:41
  8.3 0.0 collective-permute-done.1.came_ref
  8.3 0.1 select.1
  8.4 1.3 %collective-permute-start.2 = (f32[33,2,8,128]{3,2,1,0:T(8,128)S(1)}, f32[33,2,8,128]{3,2,1,0:T(8,128)S(1)}, u32[]{:S(2)}, u32[]{:S(2)}) collective-permute-start(f32[33,2,8,128]{3,2,1,0:T(8,128)S(1)} %get-tuple-element.34.kept_ref), channel_id=1, source_target_pairs={{0,16},{8,24},{16,0},{24,8},{1,17},{9,25},{17,1},{25,9},{2,18},{10... | collective-permute-start | bytes 811016 | tf_op jit(solution)/shard_map/ppermute | solution.py:41
  9.8 0.0 collective-permute-done.3.refs_1_
  9.8 2.4 %collective-permute-start.4 = (f32[3,8,128]{2,1,0:T(8,128)S(1)}, f32[3,8,128]{2,1,0:T(8,128)S(1)}, u32[]{:S(2)}, u32[]{:S(2)}) collective-permute-start(f32[3,8,128]{2,1,0:T(8,128)S(1)} %get-tuple-element.38.own_ref), channel_id=1, source_target_pairs={{0,4},{1,5},{2,6},{3,7},{4,0},{5,1},{6,2},{7,3},{8,12},{9,13},{10,... | collective-permute-start | bytes 36872 | tf_op jit(solution)/shard_map/ppermute | solution.py:41
  12.2 1.1 %collective-permute-done.4.other_ref = f32[3,8,128]{2,1,0:T(8,128)S(1)} collective-permute-done((f32[3,8,128]{2,1,0:T(8,128)S(1)}, f32[3,8,128]{2,1,0:T(8,128)S(1)}, u32[]{:S(2)}, u32[]{:S(2)}) %collective-permute-start.4) | collective-permute-done | bytes 12320 | tf_op jit(solution)/shard_map/ppermute | solution.py:41
  13.3 2.1 %collective-permute-start.5 = (f32[1,2,3,8,128]{4,3,2,1,0:T(8,128)S(1)}, f32[1,2,3,8,128]{4,3,2,1,0:T(8,128)S(1)}, u32[]{:S(2)}, u32[]{:S(2)}) collective-permute-start(f32[1,2,3,8,128]{4,3,2,1,0:T(8,128)S(1)} %join.1.rest_0_), channel_id=1, source_target_pairs={{0,8},{8,0},{16,24},{24,16},{1,9},{9,1},{17,25},{25,17},{2,10},{10... | collective-permute-start | bytes 73736 | tf_op jit(solution)/shard_map/ppermute | solution.py:41
  15.4 1.6 %collective-permute-start.6 = (f32[1,2,3,8,128]{4,3,2,1,0:T(8,128)S(1)}, f32[1,2,3,8,128]{4,3,2,1,0:T(8,128)S(1)}, u32[]{:S(2)}, u32[]{:S(2)}) collective-permute-start(f32[1,2,3,8,128]{4,3,2,1,0:T(8,128)S(1)} %join.1.rest_0_), channel_id=1, source_target_pairs={{0,16},{8,24},{16,0},{24,8},{1,17},{9,25},{17,1},{25,9},{2,18},{10... | collective-permute-start | bytes 73736 | tf_op jit(solution)/shard_map/ppermute | solution.py:41
  16.9 0.1 collective-permute-start.7
  17.1 0.0 collective-permute-done.2.came_ref
  17.1 0.4 %rotate.1.rotated_ref = f32[32,2,8,128]{3,2,1,0:T(8,128)S(1)} custom-call(s32[32]{0:T(128)S(4)} %get-tuple-element.23.shifts_ref, f32[33,2,8,128]{3,2,1,0:T(8,128)S(1)} %get-tuple-element.34.kept_ref, f32[33,2,8,128]{3,2,1,0:T(8,128)S(1)} %collective-permute-done.2.came_ref), custom_call_target="tpu_custom_call" | custom-call | flops 1048576000 | bytes 4096000 | tf_op jit(solution)/shard_map/rotate/pallas_call | solution.py:451
  17.5 0.0 collective-permute-done.5.rest_1_
  17.5 0.6 %collective-permute-done.6.rest_2_ = f32[1,2,3,8,128]{4,3,2,1,0:T(8,128)S(1)} collective-permute-done((f32[1,2,3,8,128]{4,3,2,1,0:T(8,128)S(1)}, f32[1,2,3,8,128]{4,3,2,1,0:T(8,128)S(1)}, u32[]{:S(2)}, u32[]{:S(2)}) %collective-permute-start.6) | collective-permute-done | bytes 24608 | tf_op jit(solution)/shard_map/ppermute | solution.py:41
  18.1 2.1 %collective-permute-done.7.rest_3_ = f32[1,2,3,8,128]{4,3,2,1,0:T(8,128)S(1)} collective-permute-done((f32[1,2,3,8,128]{4,3,2,1,0:T(8,128)S(1)}, f32[1,2,3,8,128]{4,3,2,1,0:T(8,128)S(1)}, u32[]{:S(2)}, u32[]{:S(2)}) %collective-permute-start.7) | collective-permute-done | bytes 24608 | tf_op jit(solution)/shard_map/ppermute | solution.py:41
  20.2 1.0 %finish.1 = f32[8,32,256]{2,1,0:T(8,128)} custom-call(s32[32]{0:T(128)S(4)} %get-tuple-element.23.shifts_ref, f32[2,32,8,128]{3,2,1,0:T(8,128)S(1)} %get-tuple-element.29.columns_ref, f32[32,2,8,128]{3,2,1,0:T(8,128)S(1)} %rotate.1.rotated_ref, f32[1,2,3,8,128]{4,3,2,1,0:T(8,128)S(1)} %join.1.rest_0_, ...), custom_call_target="tpu_custom_call" | custom-call | flops 1572864000 | bytes 6144000 | tf_op jit(solution)/shard_map/finish/pallas_call | solution.py:476
  (3 shorter events, 0.0 us)
Async XLA Ops:
  1.5 3.6 %collective-permute-start = (f32[2,3,8,128]{3,2,1,0:T(8,128)S(1)}, f32[2,3,8,128]{3,2,1,0:T(8,128)S(1)}, u32[]{:S(2)}, u32[]{:S(2)}) collective-permute-start(f32[2,3,8,128]{3,2,1,0:T(8,128)S(1)} %get-tuple-element.30.refs_0_), channel_id=1, source_target_pairs={{0,1},{1,0},{2,3},{3,2},{4,5},{5,4},{6,7},{7,6},{8,9},{9,8},{10,11... | collective-permute-start | bytes 73736 | tf_op jit(solution)/shard_map/ppermute | solution.py:41
  5.1 3.2 %collective-permute-start.1 = (f32[33,2,8,128]{3,2,1,0:T(8,128)S(1)}, f32[33,2,8,128]{3,2,1,0:T(8,128)S(1)}, u32[]{:S(2)}, u32[]{:S(2)}) collective-permute-start(f32[33,2,8,128]{3,2,1,0:T(8,128)S(1)} %get-tuple-element.33.kept_ref), channel_id=1, source_target_pairs={{0,8},{8,0},{16,24},{24,16},{1,9},{9,1},{17,25},{25,17},{2,10},{10... | collective-permute-start | bytes 811016 | tf_op jit(solution)/shard_map/ppermute | solution.py:41
  6.5 3.3 %collective-permute-start.3 = (f32[2,3,8,128]{3,2,1,0:T(8,128)S(1)}, f32[2,3,8,128]{3,2,1,0:T(8,128)S(1)}, u32[]{:S(2)}, u32[]{:S(2)}) collective-permute-start(f32[2,3,8,128]{3,2,1,0:T(8,128)S(1)} %get-tuple-element.35.refs_0_), channel_id=1, source_target_pairs={{0,2},{1,3},{2,0},{3,1},{4,6},{5,7},{6,4},{7,5},{8,10},{9,11},{10,... | collective-permute-start | bytes 73736 | tf_op jit(solution)/shard_map/ppermute | solution.py:41
  8.4 8.6 %collective-permute-start.2 = (f32[33,2,8,128]{3,2,1,0:T(8,128)S(1)}, f32[33,2,8,128]{3,2,1,0:T(8,128)S(1)}, u32[]{:S(2)}, u32[]{:S(2)}) collective-permute-start(f32[33,2,8,128]{3,2,1,0:T(8,128)S(1)} %get-tuple-element.34.kept_ref), channel_id=1, source_target_pairs={{0,16},{8,24},{16,0},{24,8},{1,17},{9,25},{17,1},{25,9},{2,18},{10... | collective-permute-start | bytes 811016 | tf_op jit(solution)/shard_map/ppermute | solution.py:41
  9.8 3.5 %collective-permute-start.4 = (f32[3,8,128]{2,1,0:T(8,128)S(1)}, f32[3,8,128]{2,1,0:T(8,128)S(1)}, u32[]{:S(2)}, u32[]{:S(2)}) collective-permute-start(f32[3,8,128]{2,1,0:T(8,128)S(1)} %get-tuple-element.38.own_ref), channel_id=1, source_target_pairs={{0,4},{1,5},{2,6},{3,7},{4,0},{5,1},{6,2},{7,3},{8,12},{9,13},{10,... | collective-permute-start | bytes 36872 | tf_op jit(solution)/shard_map/ppermute | solution.py:41
  13.3 4.2 %collective-permute-start.5 = (f32[1,2,3,8,128]{4,3,2,1,0:T(8,128)S(1)}, f32[1,2,3,8,128]{4,3,2,1,0:T(8,128)S(1)}, u32[]{:S(2)}, u32[]{:S(2)}) collective-permute-start(f32[1,2,3,8,128]{4,3,2,1,0:T(8,128)S(1)} %join.1.rest_0_), channel_id=1, source_target_pairs={{0,8},{8,0},{16,24},{24,16},{1,9},{9,1},{17,25},{25,17},{2,10},{10... | collective-permute-start | bytes 73736 | tf_op jit(solution)/shard_map/ppermute | solution.py:41
  15.4 2.8 %collective-permute-start.6 = (f32[1,2,3,8,128]{4,3,2,1,0:T(8,128)S(1)}, f32[1,2,3,8,128]{4,3,2,1,0:T(8,128)S(1)}, u32[]{:S(2)}, u32[]{:S(2)}) collective-permute-start(f32[1,2,3,8,128]{4,3,2,1,0:T(8,128)S(1)} %join.1.rest_0_), channel_id=1, source_target_pairs={{0,16},{8,24},{16,0},{24,8},{1,17},{9,25},{17,1},{25,9},{2,18},{10... | collective-permute-start | bytes 73736 | tf_op jit(solution)/shard_map/ppermute | solution.py:41
  16.9 3.3 %collective-permute-start.7 = (f32[1,2,3,8,128]{4,3,2,1,0:T(8,128)S(1)}, f32[1,2,3,8,128]{4,3,2,1,0:T(8,128)S(1)}, u32[]{:S(2)}, u32[]{:S(2)}) collective-permute-start(f32[1,2,3,8,128]{4,3,2,1,0:T(8,128)S(1)} %join.1.rest_0_), channel_id=1, source_target_pairs={{0,24},{8,16},{16,8},{24,0},{1,25},{9,17},{17,9},{25,1},{2,26},{10... | collective-permute-start | bytes 73736 | tf_op jit(solution)/shard_map/ppermute | solution.py:41

commit v5 on v4

--- a/solution.py
+++ b/solution.py
@@ -90,16 +90,18 @@
 
 def offsets_kernel(
     state_hbm, inverse_hbm, velocity_hbm, coupling_hbm, diffusivity_hbm, shifts_hbm,
-    out_ref, state_ref, inverse_ref, velocity_ref, diffusivity_ref, shifts_ref, mixing_ref,
-    coupling_ref, sems,
+    out_ref, state_ref, velocity_ref, diffusivity_ref, shifts_ref, mixing_ref,
+    first_ref, last_ref, coupling_ref, sems,
 ):
+    fields, rows, cells = state_ref.shape
     copies = [
         pltpu.make_async_copy(source, target, sems.at[i])
         for i, (source, target) in enumerate(
             (
-                (inverse_hbm, inverse_ref),
+                (inverse_hbm.at[:, :8], first_ref),
+                (inverse_hbm.at[:, rows - 8 :], last_ref),
+                (coupling_hbm, coupling_ref),
                 (velocity_hbm, velocity_ref),
-                (coupling_hbm, coupling_ref),
                 (diffusivity_hbm, diffusivity_ref),
                 (state_hbm, state_ref),
                 (shifts_hbm, shifts_ref),
@@ -109,13 +111,12 @@
     ]
     for copy in copies:
         copy.start()
-    for copy in copies[:4]:
+    for copy in copies[:5]:
         copy.wait()
-    fields, rows, cells = state_ref.shape
     span = fields * rows
     diffusivity = as_column(diffusivity_ref[...])
-    first = diffusivity * inverse_ref[:, 0, :]
-    last = diffusivity * inverse_ref[:, rows - 1, :]
+    first = diffusivity * first_ref[:, 0, :]
+    last = diffusivity * last_ref[:, 7, :]
     first = jnp.concatenate([first] * fields, axis=1)
     last = jnp.concatenate([last] * fields, axis=1)
     speed = jnp.concatenate([jnp.broadcast_to(velocity_ref[...], (fields, rows))] * fields, axis=1)
@@ -134,7 +135,7 @@
         weights.append(jnp.where(own, vector, 0.0) + 0.5 * mix * (lower - upper))
         drift.append(jnp.where(own, 0.5 * speed * vector, 0.0))
     table = jnp.concatenate(weights + drift, axis=0)
-    copies[4].wait()
+    copies[5].wait()
     sums = jnp.dot(
         table,
         state_ref[...].reshape(span, cells),
@@ -149,7 +150,7 @@
     for e in range(2):
         for j in range(width // LANES):
             out_ref[e, j] = tile(total[e * fields : (e + 1) * fields], j)
-    for copy in copies[5:]:
+    for copy in copies[6:]:
         copy.wait()
 
 
@@ -278,16 +279,14 @@
             out_ref[r, 1 - swap] = value[1]
 
 
-def finish_kernel(count, parts, shifts_ref, columns_ref, rotated_ref, *rest):
-    out_hbm, forcing_ref, total_ref, sems = rest[parts:]
+def finish_kernel(count, starts, shifts_ref, columns_ref, rotated_ref, *rest):
+    out_hbm, forcing_ref, total_ref, sems = rest[len(starts) :]
     rows, tiles, fields, lanes = rotated_ref.shape
     cells = tiles * lanes
-    at = 0
     place = lax.axis_index("az")
     lane = iota((fields, lanes), 1)
-    for part in rest[:parts]:
+    for at, part in zip(reversed(starts), rest):
         forcing_ref[at : at + part.shape[0]] = part[...]
-        at += part.shape[0]
     for m in range(count):
         before = (((place ^ m) - 1) & (count - 1)) ^ place
         after = (((place ^ m) + 1) & (count - 1)) ^ place
@@ -396,22 +395,23 @@
     assert tiles == 2 and fields == 8 and 2 * rows <= LANES
     count = lax.axis_size("az")
     segments = lax.axis_size("rad")
-    offsets, state_near, inverse_near, velocity, diffusivity, shifts, mixing = pl.pallas_call(
+    offsets, state_near, velocity, diffusivity, shifts, mixing = pl.pallas_call(
         offsets_kernel,
         out_shape=[
             pltpu.VMEM((2, tiles + 1, fields, LANES), f32),
             pltpu.VMEM(state.shape, f32),
-            pltpu.VMEM(inverse.shape, f32),
             pltpu.VMEM((1, rows), f32),
             pltpu.VMEM((1, fields), f32),
             pltpu.SMEM(shifts.shape, jnp.int32),
             pltpu.SMEM(coupling.shape, f32),
         ],
         in_specs=[ANY] * 6,
-        out_specs=[VMEM] * 5 + [SMEM] * 2,
+        out_specs=[VMEM] * 4 + [SMEM] * 2,
         scratch_shapes=[
+            pltpu.VMEM((fields, 8, rows), f32),
+            pltpu.VMEM((fields, 8, rows), f32),
             pltpu.VMEM((fields, fields), f32),
-            pltpu.SemaphoreType.DMA((7,)),
+            pltpu.SemaphoreType.DMA((8,)),
         ],
         cost_estimate=cost(5000),
         name="offsets",
@@ -435,7 +435,7 @@
         ],
         cost_estimate=cost(8000),
         name="solve",
-    )(in_smem(mixing), *map(in_vmem, (state_near, velocity, diffusivity, inverse_near)))
+    )(in_smem(mixing), *map(in_vmem, (state_near, velocity, diffusivity, inverse)))
     kept, held, sums = merge(0, offsets, coeffs, solved)
     bit = 1
     while 2 * bit < count:
@@ -473,8 +473,9 @@
         ours = parts[0] if len(parts) == 1 else jnp.concatenate(parts, 0)
         parts += [swapped(ours, "az", i * bit) for i in range(1, min(4, count // bit))]
         bit *= 4
+    starts = [sum(x.shape[0] for x in parts[:i]) for i in range(len(parts))]
     out = pl.pallas_call(
-        functools.partial(finish_kernel, count, len(parts)),
+        functools.partial(finish_kernel, count, starts),
         out_shape=jax.ShapeDtypeStruct(state.shape, f32),
         in_specs=[SMEM] + [VMEM] * (2 + len(parts)),
         out_specs=ANY,
@@ -485,7 +486,7 @@
         ],
         cost_estimate=cost(6000),
         name="finish",
-    )(shifts, in_vmem(columns), in_vmem(rotated), *map(in_vmem, parts))
+    )(shifts, in_vmem(columns), in_vmem(rotated), *map(in_vmem, reversed(parts)))
     return out[:, None]
 
 

time: 21.7 us -> 20.6 us (0.949); the launches traced: 21.2 us -> 20.5 us
  waiting for transfers between devices: 3.82 us -> 2.91 us
    ppermute x8, waiting for transfers between devices: 3.82 us -> 2.91 us  [swapped(): lax.ppermute(block, axis, [(i, i ^ bit) for i in range(lax.axis_size(axis...]
  transfers between devices with their start and end apart: 8 -> 8, of which waited for: 3 -> 3; matrix products, arithmetic and copies ran while one was open for 0% -> 0% of each run, Pallas kernels for 9% -> 10%
where the time goes in v5:
time: 20.6 us; the launch traced here: 20.5 us
  starting transfers between devices  12.9 us (63%)
  Pallas kernels  4.57 us (22%)
  waiting for transfers between devices  2.91 us (14%)
    ppermute x8, starting transfers between devices, swapped(): lax.ppermute(block, axis, [(i, i ^ bit) for i in range(lax.axis_size(axis...  12.9 us
    ppermute x8, waiting for transfers between devices, swapped(): lax.ppermute(block, axis, [(i, i ^ bit) for i in range(lax.axis_size(axis...  2.91 us
    pallas_call x1, Pallas kernels, per_device(): pl.pallas_call(offsets_kernel, out_shape=[pltpu.VMEM((2, tiles + 1, field...  1.47 us
    pallas_call x1, Pallas kernels, per_device(): pl.pallas_call(functools.partial(solve_kernel, count, segments), out_shap...  1.47 us
    pallas_call x1, Pallas kernels, per_device(): pl.pallas_call(functools.partial(finish_kernel, count, starts), out_shape...  1.05 us
    pallas_call x1, Pallas kernels, per_device(): pl.pallas_call(functools.partial(rotate_kernel, count, bit), out_shape=pl...  0.44 us
  transfers between devices with their start and end apart: 8, of which 3 were waited for; matrix products, arithmetic and copies ran while one was open for 0% of the time, Pallas kernels for 10%

profile of v5, /device:TPU:1, one launch (start us, length us, event | category | flops | bytes accessed | tf_op | source)
XLA Modules:
  0.0 20.5 jit_solution(4421569774912948312)
XLA Ops:
  0.0 0.0 copy-start
  0.0 1.5 %offsets.1 = (f32[2,3,8,128]{3,2,1,0:T(8,128)S(1)}, f32[8,32,256]{2,1,0:T(8,128)S(1)}, f32[1,32]{1,0:T(1,128)S(1)}, f32[1,8]{1,0:T(1,128)S(1)}, s32[32]{0:T(128)S(4)}, /*index=5*/f32[8,8]{1,0:T(8,128)S(4)}) custom-call(f32[8,32,256]{2,1,0:T(8,128)} %bitcast.6, f32[8,32,32]{2,1,0:T(8,128)} %inverse_ref.1, f32[1,32]{1,0:T(1,128)} %bitcast.7, ...), custom_call_target="tpu_custom_call" | custom-call | flops 1310720000 | bytes 5120000 | tf_op jit(solution)/shard_map/offsets/pallas_call | solution.py:398
  1.5 2.1 %collective-permute-start = (f32[2,3,8,128]{3,2,1,0:T(8,128)S(1)}, f32[2,3,8,128]{3,2,1,0:T(8,128)S(1)}, u32[]{:S(2)}, u32[]{:S(2)}) collective-permute-start(f32[2,3,8,128]{3,2,1,0:T(8,128)S(1)} %get-tuple-element.28.refs_0_), channel_id=1, source_target_pairs={{0,1},{1,0},{2,3},{3,2},{4,5},{5,4},{6,7},{7,6},{8,9},{9,8},{10,11... | collective-permute-start | bytes 73736 | tf_op jit(solution)/shard_map/ppermute | solution.py:41
  3.6 0.0 copy-done
  3.6 1.5 %solve.1 = (f32[33,2,8,128]{3,2,1,0:T(8,128)S(1)}, f32[2,32,8,128]{3,2,1,0:T(8,128)S(1)}, f32[14,8,128]{2,1,0:T(8,128)S(1)}, f32[4,8,128]{2,1,0:T(8,128)S(1)}) custom-call(f32[8,8]{1,0:T(8,128)S(4)} %get-tuple-element.23.coupling_ref, f32[8,32,256]{2,1,0:T(8,128)S(1)} %get-tuple-element.24.state_ref, f32[1,32]{1,0:T(1,128)S(1)} %get-tuple-element.25.velocity_ref, ...), custom_call_target="tpu_custom_call" | custom-call | flops 2097152000 | bytes 8192000 | tf_op jit(solution)/shard_map/solve/pallas_call | solution.py:421
  5.1 0.0 collective-permute-done.refs_1_
  5.1 1.3 %collective-permute-start.1 = (f32[33,2,8,128]{3,2,1,0:T(8,128)S(1)}, f32[33,2,8,128]{3,2,1,0:T(8,128)S(1)}, u32[]{:S(2)}, u32[]{:S(2)}) collective-permute-start(f32[33,2,8,128]{3,2,1,0:T(8,128)S(1)} %get-tuple-element.31.kept_ref), channel_id=1, source_target_pairs={{0,8},{8,0},{16,24},{24,16},{1,9},{9,1},{17,25},{25,17},{2,10},{10... | collective-permute-start | bytes 811016 | tf_op jit(solution)/shard_map/ppermute | solution.py:41
  6.4 1.8 %collective-permute-start.3 = (f32[2,3,8,128]{3,2,1,0:T(8,128)S(1)}, f32[2,3,8,128]{3,2,1,0:T(8,128)S(1)}, u32[]{:S(2)}, u32[]{:S(2)}) collective-permute-start(f32[2,3,8,128]{3,2,1,0:T(8,128)S(1)} %get-tuple-element.33.refs_0_), channel_id=1, source_target_pairs={{0,2},{1,3},{2,0},{3,1},{4,6},{5,7},{6,4},{7,5},{8,10},{9,11},{10,... | collective-permute-start | bytes 73736 | tf_op jit(solution)/shard_map/ppermute | solution.py:41
  8.3 0.0 collective-permute-done.1.came_ref
  8.3 0.1 select.1
  8.4 1.3 %collective-permute-start.2 = (f32[33,2,8,128]{3,2,1,0:T(8,128)S(1)}, f32[33,2,8,128]{3,2,1,0:T(8,128)S(1)}, u32[]{:S(2)}, u32[]{:S(2)}) collective-permute-start(f32[33,2,8,128]{3,2,1,0:T(8,128)S(1)} %get-tuple-element.32.kept_ref), channel_id=1, source_target_pairs={{0,16},{8,24},{16,0},{24,8},{1,17},{9,25},{17,1},{25,9},{2,18},{10... | collective-permute-start | bytes 811016 | tf_op jit(solution)/shard_map/ppermute | solution.py:41
  9.7 0.0 collective-permute-done.3.refs_1_
  9.7 2.4 %collective-permute-start.4 = (f32[3,8,128]{2,1,0:T(8,128)S(1)}, f32[3,8,128]{2,1,0:T(8,128)S(1)}, u32[]{:S(2)}, u32[]{:S(2)}) collective-permute-start(f32[3,8,128]{2,1,0:T(8,128)S(1)} %get-tuple-element.36.own_ref), channel_id=1, source_target_pairs={{0,4},{1,5},{2,6},{3,7},{4,0},{5,1},{6,2},{7,3},{8,12},{9,13},{10,... | collective-permute-start | bytes 36872 | tf_op jit(solution)/shard_map/ppermute | solution.py:41
  12.1 1.1 %collective-permute-done.4.other_ref = f32[3,8,128]{2,1,0:T(8,128)S(1)} collective-permute-done((f32[3,8,128]{2,1,0:T(8,128)S(1)}, f32[3,8,128]{2,1,0:T(8,128)S(1)}, u32[]{:S(2)}, u32[]{:S(2)}) %collective-permute-start.4) | collective-permute-done | bytes 12320 | tf_op jit(solution)/shard_map/ppermute | solution.py:41
  13.2 3.5 %collective-permute-start.5 = (f32[1,2,3,8,128]{4,3,2,1,0:T(8,128)S(1)}, f32[1,2,3,8,128]{4,3,2,1,0:T(8,128)S(1)}, u32[]{:S(2)}, u32[]{:S(2)}) collective-permute-start(f32[1,2,3,8,128]{4,3,2,1,0:T(8,128)S(1)} %join.1.rest_3_), channel_id=1, source_target_pairs={{0,24},{8,16},{16,8},{24,0},{1,25},{9,17},{17,9},{25,1},{2,26},{10... | collective-permute-start | bytes 73736 | tf_op jit(solution)/shard_map/ppermute | solution.py:41
  16.8 0.0 collective-permute-start.6
  16.8 0.5 %collective-permute-start.7 = (f32[1,2,3,8,128]{4,3,2,1,0:T(8,128)S(1)}, f32[1,2,3,8,128]{4,3,2,1,0:T(8,128)S(1)}, u32[]{:S(2)}, u32[]{:S(2)}) collective-permute-start(f32[1,2,3,8,128]{4,3,2,1,0:T(8,128)S(1)} %join.1.rest_3_), channel_id=1, source_target_pairs={{0,8},{8,0},{16,24},{24,16},{1,9},{9,1},{17,25},{25,17},{2,10},{10... | collective-permute-start | bytes 73736 | tf_op jit(solution)/shard_map/ppermute | solution.py:41
  17.2 0.0 collective-permute-done.2.came_ref
  17.2 0.4 %rotate.1.rotated_ref = f32[32,2,8,128]{3,2,1,0:T(8,128)S(1)} custom-call(s32[32]{0:T(128)S(4)} %get-tuple-element.22.shifts_ref, f32[33,2,8,128]{3,2,1,0:T(8,128)S(1)} %get-tuple-element.32.kept_ref, f32[33,2,8,128]{3,2,1,0:T(8,128)S(1)} %collective-permute-done.2.came_ref), custom_call_target="tpu_custom_call" | custom-call | flops 1048576000 | bytes 4096000 | tf_op jit(solution)/shard_map/rotate/pallas_call | solution.py:451
  17.7 0.6 %collective-permute-done.5.rest_0_ = f32[1,2,3,8,128]{4,3,2,1,0:T(8,128)S(1)} collective-permute-done((f32[1,2,3,8,128]{4,3,2,1,0:T(8,128)S(1)}, f32[1,2,3,8,128]{4,3,2,1,0:T(8,128)S(1)}, u32[]{:S(2)}, u32[]{:S(2)}) %collective-permute-start.5) | collective-permute-done | bytes 24608 | tf_op jit(solution)/shard_map/ppermute | solution.py:41
  18.3 1.2 %collective-permute-done.6.rest_1_ = f32[1,2,3,8,128]{4,3,2,1,0:T(8,128)S(1)} collective-permute-done((f32[1,2,3,8,128]{4,3,2,1,0:T(8,128)S(1)}, f32[1,2,3,8,128]{4,3,2,1,0:T(8,128)S(1)}, u32[]{:S(2)}, u32[]{:S(2)}) %collective-permute-start.6) | collective-permute-done | bytes 24608 | tf_op jit(solution)/shard_map/ppermute | solution.py:41
  19.4 0.0 collective-permute-done.7.rest_2_
  19.4 1.0 %finish.1 = f32[8,32,256]{2,1,0:T(8,128)} custom-call(s32[32]{0:T(128)S(4)} %get-tuple-element.22.shifts_ref, f32[2,32,8,128]{3,2,1,0:T(8,128)S(1)} %get-tuple-element.27.columns_ref, f32[32,2,8,128]{3,2,1,0:T(8,128)S(1)} %rotate.1.rotated_ref, f32[1,2,3,8,128]{4,3,2,1,0:T(8,128)S(1)} %collective-permute-done.5.rest_0_, ...), custom_call_target="tpu_custom_call" | custom-call | flops 1572864000 | bytes 6144000 | tf_op jit(solution)/shard_map/finish/pallas_call | solution.py:477
  (3 shorter events, 0.0 us)
Async XLA Ops:
  0.0 3.6 %copy-start = (f32[8,32,32]{2,1,0:T(8,128)S(1)}, f32[8,32,32]{2,1,0:T(8,128)}, u32[]{:S(2)}) copy-start(f32[8,32,32]{2,1,0:T(8,128)} %inverse_ref.1) | copy-start | bytes 98308
  1.5 3.6 %collective-permute-start = (f32[2,3,8,128]{3,2,1,0:T(8,128)S(1)}, f32[2,3,8,128]{3,2,1,0:T(8,128)S(1)}, u32[]{:S(2)}, u32[]{:S(2)}) collective-permute-start(f32[2,3,8,128]{3,2,1,0:T(8,128)S(1)} %get-tuple-element.28.refs_0_), channel_id=1, source_target_pairs={{0,1},{1,0},{2,3},{3,2},{4,5},{5,4},{6,7},{7,6},{8,9},{9,8},{10,11... | collective-permute-start | bytes 73736 | tf_op jit(solution)/shard_map/ppermute | solution.py:41
  5.1 3.2 %collective-permute-start.1 = (f32[33,2,8,128]{3,2,1,0:T(8,128)S(1)}, f32[33,2,8,128]{3,2,1,0:T(8,128)S(1)}, u32[]{:S(2)}, u32[]{:S(2)}) collective-permute-start(f32[33,2,8,128]{3,2,1,0:T(8,128)S(1)} %get-tuple-element.31.kept_ref), channel_id=1, source_target_pairs={{0,8},{8,0},{16,24},{24,16},{1,9},{9,1},{17,25},{25,17},{2,10},{10... | collective-permute-start | bytes 811016 | tf_op jit(solution)/shard_map/ppermute | solution.py:41
  6.4 3.3 %collective-permute-start.3 = (f32[2,3,8,128]{3,2,1,0:T(8,128)S(1)}, f32[2,3,8,128]{3,2,1,0:T(8,128)S(1)}, u32[]{:S(2)}, u32[]{:S(2)}) collective-permute-start(f32[2,3,8,128]{3,2,1,0:T(8,128)S(1)} %get-tuple-element.33.refs_0_), channel_id=1, source_target_pairs={{0,2},{1,3},{2,0},{3,1},{4,6},{5,7},{6,4},{7,5},{8,10},{9,11},{10,... | collective-permute-start | bytes 73736 | tf_op jit(solution)/shard_map/ppermute | solution.py:41
  8.4 8.8 %collective-permute-start.2 = (f32[33,2,8,128]{3,2,1,0:T(8,128)S(1)}, f32[33,2,8,128]{3,2,1,0:T(8,128)S(1)}, u32[]{:S(2)}, u32[]{:S(2)}) collective-permute-start(f32[33,2,8,128]{3,2,1,0:T(8,128)S(1)} %get-tuple-element.32.kept_ref), channel_id=1, source_target_pairs={{0,16},{8,24},{16,0},{24,8},{1,17},{9,25},{17,1},{25,9},{2,18},{10... | collective-permute-start | bytes 811016 | tf_op jit(solution)/shard_map/ppermute | solution.py:41
  9.7 3.5 %collective-permute-start.4 = (f32[3,8,128]{2,1,0:T(8,128)S(1)}, f32[3,8,128]{2,1,0:T(8,128)S(1)}, u32[]{:S(2)}, u32[]{:S(2)}) collective-permute-start(f32[3,8,128]{2,1,0:T(8,128)S(1)} %get-tuple-element.36.own_ref), channel_id=1, source_target_pairs={{0,4},{1,5},{2,6},{3,7},{4,0},{5,1},{6,2},{7,3},{8,12},{9,13},{10,... | collective-permute-start | bytes 36872 | tf_op jit(solution)/shard_map/ppermute | solution.py:41
  13.2 5.0 %collective-permute-start.5 = (f32[1,2,3,8,128]{4,3,2,1,0:T(8,128)S(1)}, f32[1,2,3,8,128]{4,3,2,1,0:T(8,128)S(1)}, u32[]{:S(2)}, u32[]{:S(2)}) collective-permute-start(f32[1,2,3,8,128]{4,3,2,1,0:T(8,128)S(1)} %join.1.rest_3_), channel_id=1, source_target_pairs={{0,24},{8,16},{16,8},{24,0},{1,25},{9,17},{17,9},{25,1},{2,26},{10... | collective-permute-start | bytes 73736 | tf_op jit(solution)/shard_map/ppermute | solution.py:41
  16.8 2.7 %collective-permute-start.6 = (f32[1,2,3,8,128]{4,3,2,1,0:T(8,128)S(1)}, f32[1,2,3,8,128]{4,3,2,1,0:T(8,128)S(1)}, u32[]{:S(2)}, u32[]{:S(2)}) collective-permute-start(f32[1,2,3,8,128]{4,3,2,1,0:T(8,128)S(1)} %join.1.rest_3_), channel_id=1, source_target_pairs={{0,16},{8,24},{16,0},{24,8},{1,17},{9,25},{17,1},{25,9},{2,18},{10... | collective-permute-start | bytes 73736 | tf_op jit(solution)/shard_map/ppermute | solution.py:41
  16.8 2.7 %collective-permute-start.7 = (f32[1,2,3,8,128]{4,3,2,1,0:T(8,128)S(1)}, f32[1,2,3,8,128]{4,3,2,1,0:T(8,128)S(1)}, u32[]{:S(2)}, u32[]{:S(2)}) collective-permute-start(f32[1,2,3,8,128]{4,3,2,1,0:T(8,128)S(1)} %join.1.rest_3_), channel_id=1, source_target_pairs={{0,8},{8,0},{16,24},{24,16},{1,9},{9,1},{17,25},{25,17},{2,10},{10... | collective-permute-start | bytes 73736 | tf_op jit(solution)/shard_map/ppermute | solution.py:41

commit v6 on v5

--- a/solution.py
+++ b/solution.py
@@ -280,19 +280,23 @@
 
 
 def finish_kernel(count, starts, shifts_ref, columns_ref, rotated_ref, *rest):
-    out_hbm, forcing_ref, total_ref, sems = rest[len(starts) :]
+    out_hbm, ghosts_ref, forcing_ref, total_ref, sems = rest[len(starts) :]
     rows, tiles, fields, lanes = rotated_ref.shape
     cells = tiles * lanes
     place = lax.axis_index("az")
     lane = iota((fields, lanes), 1)
     for at, part in zip(reversed(starts), rest):
-        forcing_ref[at : at + part.shape[0]] = part[...]
-    for m in range(count):
-        before = (((place ^ m) - 1) & (count - 1)) ^ place
-        after = (((place ^ m) + 1) & (count - 1)) ^ place
-        for e in range(2):
-            forcing_ref[m, e, 0] += jnp.where(lane == 0, forcing_ref[before, e, tiles], 0.0)
-            forcing_ref[m, e, 1] += jnp.where(lane == lanes - 1, forcing_ref[after, e, tiles], 0.0)
+        ghosts_ref[at : at + part.shape[0]] = part[:, :, tiles]
+    for at, part in zip(reversed(starts), rest):
+        for i in range(part.shape[0]):
+            own = place ^ (at + i)
+            before = ((own - 1) & (count - 1)) ^ place
+            after = ((own + 1) & (count - 1)) ^ place
+            for e in range(2):
+                low = jnp.where(lane == 0, ghosts_ref[before, e], 0.0)
+                high = jnp.where(lane == lanes - 1, ghosts_ref[after, e], 0.0)
+                forcing_ref[at + i, e, 0] = part[i, e, 0] + low
+                forcing_ref[at + i, e, 1] = part[i, e, 1] + high
     copies = []
     for batch in range(0, rows, BATCH):
         values = []
@@ -417,7 +421,7 @@
         name="offsets",
     )(state, inverse, velocity[None], coupling, diffusivity[None], shifts)
     shifts = in_smem(shifts)
-    spare = count * 2 * rows // cells
+    spare = -(-count * 2 * rows // cells)
     solved, columns, coeffs, final = pl.pallas_call(
         functools.partial(solve_kernel, count, segments),
         out_shape=[
@@ -480,7 +484,8 @@
         in_specs=[SMEM] + [VMEM] * (2 + len(parts)),
         out_specs=ANY,
         scratch_shapes=[
-            pltpu.VMEM((count, 2, tiles + 1, fields, LANES), f32),
+            pltpu.VMEM((count, 2, fields, LANES), f32),
+            pltpu.VMEM((count, 2, tiles, fields, LANES), f32),
             pltpu.VMEM((rows // BATCH, tiles, BATCH * fields, LANES), f32),
             pltpu.SemaphoreType.DMA((rows // BATCH, tiles)),
         ],

time: 20.6 us -> 20.6 us (level)
  no operation moved by 1% of the time
where the time goes in v6:
time: 20.6 us; the launch traced here: 20.4 us
  starting transfers between devices  12.9 us (63%)
  Pallas kernels  4.52 us (22%)
  waiting for transfers between devices  2.91 us (14%)
    ppermute x8, starting transfers between devices, swapped(): lax.ppermute(block, axis, [(i, i ^ bit) for i in range(lax.axis_size(axis...  12.9 us
    ppermute x8, waiting for transfers between devices, swapped(): lax.ppermute(block, axis, [(i, i ^ bit) for i in range(lax.axis_size(axis...  2.91 us
    pallas_call x1, Pallas kernels, per_device(): pl.pallas_call(offsets_kernel, out_shape=[pltpu.VMEM((2, tiles + 1, field...  1.47 us
    pallas_call x1, Pallas kernels, per_device(): pl.pallas_call(functools.partial(solve_kernel, count, segments), out_shap...  1.47 us
    pallas_call x1, Pallas kernels, per_device(): pl.pallas_call(functools.partial(finish_kernel, count, starts), out_shape...  0.99 us
    pallas_call x1, Pallas kernels, per_device(): pl.pallas_call(functools.partial(rotate_kernel, count, bit), out_shape=pl...  0.44 us
  transfers between devices with their start and end apart: 8, of which 3 were waited for; matrix products, arithmetic and copies ran while one was open for 0% of the time, Pallas kernels for 10%

profile of v6, /device:TPU:1, one launch (start us, length us, event | category | flops | bytes accessed | tf_op | source)
XLA Modules:
  0.0 20.4 jit_solution(4762840284185482091)
XLA Ops:
  0.0 0.0 copy-start
  0.0 1.5 %offsets.1 = (f32[2,3,8,128]{3,2,1,0:T(8,128)S(1)}, f32[8,32,256]{2,1,0:T(8,128)S(1)}, f32[1,32]{1,0:T(1,128)S(1)}, f32[1,8]{1,0:T(1,128)S(1)}, s32[32]{0:T(128)S(4)}, /*index=5*/f32[8,8]{1,0:T(8,128)S(4)}) custom-call(f32[8,32,256]{2,1,0:T(8,128)} %bitcast.6, f32[8,32,32]{2,1,0:T(8,128)} %inverse_ref.1, f32[1,32]{1,0:T(1,128)} %bitcast.7, ...), custom_call_target="tpu_custom_call" | custom-call | flops 1310720000 | bytes 5120000 | tf_op jit(solution)/shard_map/offsets/pallas_call | solution.py:402
  1.5 2.1 %collective-permute-start = (f32[2,3,8,128]{3,2,1,0:T(8,128)S(1)}, f32[2,3,8,128]{3,2,1,0:T(8,128)S(1)}, u32[]{:S(2)}, u32[]{:S(2)}) collective-permute-start(f32[2,3,8,128]{3,2,1,0:T(8,128)S(1)} %get-tuple-element.28.refs_0_), channel_id=1, source_target_pairs={{0,1},{1,0},{2,3},{3,2},{4,5},{5,4},{6,7},{7,6},{8,9},{9,8},{10,11... | collective-permute-start | bytes 73736 | tf_op jit(solution)/shard_map/ppermute | solution.py:41
  3.6 0.0 copy-done
  3.6 1.5 %solve.1 = (f32[33,2,8,128]{3,2,1,0:T(8,128)S(1)}, f32[2,32,8,128]{3,2,1,0:T(8,128)S(1)}, f32[14,8,128]{2,1,0:T(8,128)S(1)}, f32[4,8,128]{2,1,0:T(8,128)S(1)}) custom-call(f32[8,8]{1,0:T(8,128)S(4)} %get-tuple-element.23.coupling_ref, f32[8,32,256]{2,1,0:T(8,128)S(1)} %get-tuple-element.24.state_ref, f32[1,32]{1,0:T(1,128)S(1)} %get-tuple-element.25.velocity_ref, ...), custom_call_target="tpu_custom_call" | custom-call | flops 2097152000 | bytes 8192000 | tf_op jit(solution)/shard_map/solve/pallas_call | solution.py:425
  5.1 0.0 collective-permute-done.refs_1_
  5.1 1.3 %collective-permute-start.1 = (f32[33,2,8,128]{3,2,1,0:T(8,128)S(1)}, f32[33,2,8,128]{3,2,1,0:T(8,128)S(1)}, u32[]{:S(2)}, u32[]{:S(2)}) collective-permute-start(f32[33,2,8,128]{3,2,1,0:T(8,128)S(1)} %get-tuple-element.31.kept_ref), channel_id=1, source_target_pairs={{0,8},{8,0},{16,24},{24,16},{1,9},{9,1},{17,25},{25,17},{2,10},{10... | collective-permute-start | bytes 811016 | tf_op jit(solution)/shard_map/ppermute | solution.py:41
  6.4 1.8 %collective-permute-start.3 = (f32[2,3,8,128]{3,2,1,0:T(8,128)S(1)}, f32[2,3,8,128]{3,2,1,0:T(8,128)S(1)}, u32[]{:S(2)}, u32[]{:S(2)}) collective-permute-start(f32[2,3,8,128]{3,2,1,0:T(8,128)S(1)} %get-tuple-element.33.refs_0_), channel_id=1, source_target_pairs={{0,2},{1,3},{2,0},{3,1},{4,6},{5,7},{6,4},{7,5},{8,10},{9,11},{10,... | collective-permute-start | bytes 73736 | tf_op jit(solution)/shard_map/ppermute | solution.py:41
  8.3 0.0 collective-permute-done.1.came_ref
  8.3 0.1 select.1
  8.4 1.3 %collective-permute-start.2 = (f32[33,2,8,128]{3,2,1,0:T(8,128)S(1)}, f32[33,2,8,128]{3,2,1,0:T(8,128)S(1)}, u32[]{:S(2)}, u32[]{:S(2)}) collective-permute-start(f32[33,2,8,128]{3,2,1,0:T(8,128)S(1)} %get-tuple-element.32.kept_ref), channel_id=1, source_target_pairs={{0,16},{8,24},{16,0},{24,8},{1,17},{9,25},{17,1},{25,9},{2,18},{10... | collective-permute-start | bytes 811016 | tf_op jit(solution)/shard_map/ppermute | solution.py:41
  9.7 0.0 collective-permute-done.3.refs_1_
  9.7 2.4 %collective-permute-start.4 = (f32[3,8,128]{2,1,0:T(8,128)S(1)}, f32[3,8,128]{2,1,0:T(8,128)S(1)}, u32[]{:S(2)}, u32[]{:S(2)}) collective-permute-start(f32[3,8,128]{2,1,0:T(8,128)S(1)} %get-tuple-element.36.own_ref), channel_id=1, source_target_pairs={{0,4},{1,5},{2,6},{3,7},{4,0},{5,1},{6,2},{7,3},{8,12},{9,13},{10,... | collective-permute-start | bytes 36872 | tf_op jit(solution)/shard_map/ppermute | solution.py:41
  12.1 1.1 %collective-permute-done.4.other_ref = f32[3,8,128]{2,1,0:T(8,128)S(1)} collective-permute-done((f32[3,8,128]{2,1,0:T(8,128)S(1)}, f32[3,8,128]{2,1,0:T(8,128)S(1)}, u32[]{:S(2)}, u32[]{:S(2)}) %collective-permute-start.4) | collective-permute-done | bytes 12320 | tf_op jit(solution)/shard_map/ppermute | solution.py:41
  13.2 3.5 %collective-permute-start.5 = (f32[1,2,3,8,128]{4,3,2,1,0:T(8,128)S(1)}, f32[1,2,3,8,128]{4,3,2,1,0:T(8,128)S(1)}, u32[]{:S(2)}, u32[]{:S(2)}) collective-permute-start(f32[1,2,3,8,128]{4,3,2,1,0:T(8,128)S(1)} %join.1.rest_3_), channel_id=1, source_target_pairs={{0,24},{8,16},{16,8},{24,0},{1,25},{9,17},{17,9},{25,1},{2,26},{10... | collective-permute-start | bytes 73736 | tf_op jit(solution)/shard_map/ppermute | solution.py:41
  16.8 0.0 collective-permute-start.6
  16.8 0.5 %collective-permute-start.7 = (f32[1,2,3,8,128]{4,3,2,1,0:T(8,128)S(1)}, f32[1,2,3,8,128]{4,3,2,1,0:T(8,128)S(1)}, u32[]{:S(2)}, u32[]{:S(2)}) collective-permute-start(f32[1,2,3,8,128]{4,3,2,1,0:T(8,128)S(1)} %join.1.rest_3_), channel_id=1, source_target_pairs={{0,8},{8,0},{16,24},{24,16},{1,9},{9,1},{17,25},{25,17},{2,10},{10... | collective-permute-start | bytes 73736 | tf_op jit(solution)/shard_map/ppermute | solution.py:41
  17.2 0.0 collective-permute-done.2.came_ref
  17.2 0.4 %rotate.1.rotated_ref = f32[32,2,8,128]{3,2,1,0:T(8,128)S(1)} custom-call(s32[32]{0:T(128)S(4)} %get-tuple-element.22.shifts_ref, f32[33,2,8,128]{3,2,1,0:T(8,128)S(1)} %get-tuple-element.32.kept_ref, f32[33,2,8,128]{3,2,1,0:T(8,128)S(1)} %collective-permute-done.2.came_ref), custom_call_target="tpu_custom_call" | custom-call | flops 1048576000 | bytes 4096000 | tf_op jit(solution)/shard_map/rotate/pallas_call | solution.py:455
  17.7 0.6 %collective-permute-done.5.rest_0_ = f32[1,2,3,8,128]{4,3,2,1,0:T(8,128)S(1)} collective-permute-done((f32[1,2,3,8,128]{4,3,2,1,0:T(8,128)S(1)}, f32[1,2,3,8,128]{4,3,2,1,0:T(8,128)S(1)}, u32[]{:S(2)}, u32[]{:S(2)}) %collective-permute-start.5) | collective-permute-done | bytes 24608 | tf_op jit(solution)/shard_map/ppermute | solution.py:41
  18.3 1.2 %collective-permute-done.6.rest_1_ = f32[1,2,3,8,128]{4,3,2,1,0:T(8,128)S(1)} collective-permute-done((f32[1,2,3,8,128]{4,3,2,1,0:T(8,128)S(1)}, f32[1,2,3,8,128]{4,3,2,1,0:T(8,128)S(1)}, u32[]{:S(2)}, u32[]{:S(2)}) %collective-permute-start.6) | collective-permute-done | bytes 24608 | tf_op jit(solution)/shard_map/ppermute | solution.py:41
  19.4 0.0 collective-permute-done.7.rest_2_
  19.4 1.0 %finish.1 = f32[8,32,256]{2,1,0:T(8,128)} custom-call(s32[32]{0:T(128)S(4)} %get-tuple-element.22.shifts_ref, f32[2,32,8,128]{3,2,1,0:T(8,128)S(1)} %get-tuple-element.27.columns_ref, f32[32,2,8,128]{3,2,1,0:T(8,128)S(1)} %rotate.1.rotated_ref, f32[1,2,3,8,128]{4,3,2,1,0:T(8,128)S(1)} %collective-permute-done.5.rest_0_, ...), custom_call_target="tpu_custom_call" | custom-call | flops 1572864000 | bytes 6144000 | tf_op jit(solution)/shard_map/finish/pallas_call | solution.py:481
  (3 shorter events, 0.0 us)
Async XLA Ops:
  0.0 3.6 %copy-start = (f32[8,32,32]{2,1,0:T(8,128)S(1)}, f32[8,32,32]{2,1,0:T(8,128)}, u32[]{:S(2)}) copy-start(f32[8,32,32]{2,1,0:T(8,128)} %inverse_ref.1) | copy-start | bytes 98308
  1.5 3.6 %collective-permute-start = (f32[2,3,8,128]{3,2,1,0:T(8,128)S(1)}, f32[2,3,8,128]{3,2,1,0:T(8,128)S(1)}, u32[]{:S(2)}, u32[]{:S(2)}) collective-permute-start(f32[2,3,8,128]{3,2,1,0:T(8,128)S(1)} %get-tuple-element.28.refs_0_), channel_id=1, source_target_pairs={{0,1},{1,0},{2,3},{3,2},{4,5},{5,4},{6,7},{7,6},{8,9},{9,8},{10,11... | collective-permute-start | bytes 73736 | tf_op jit(solution)/shard_map/ppermute | solution.py:41
  5.1 3.2 %collective-permute-start.1 = (f32[33,2,8,128]{3,2,1,0:T(8,128)S(1)}, f32[33,2,8,128]{3,2,1,0:T(8,128)S(1)}, u32[]{:S(2)}, u32[]{:S(2)}) collective-permute-start(f32[33,2,8,128]{3,2,1,0:T(8,128)S(1)} %get-tuple-element.31.kept_ref), channel_id=1, source_target_pairs={{0,8},{8,0},{16,24},{24,16},{1,9},{9,1},{17,25},{25,17},{2,10},{10... | collective-permute-start | bytes 811016 | tf_op jit(solution)/shard_map/ppermute | solution.py:41
  6.4 3.3 %collective-permute-start.3 = (f32[2,3,8,128]{3,2,1,0:T(8,128)S(1)}, f32[2,3,8,128]{3,2,1,0:T(8,128)S(1)}, u32[]{:S(2)}, u32[]{:S(2)}) collective-permute-start(f32[2,3,8,128]{3,2,1,0:T(8,128)S(1)} %get-tuple-element.33.refs_0_), channel_id=1, source_target_pairs={{0,2},{1,3},{2,0},{3,1},{4,6},{5,7},{6,4},{7,5},{8,10},{9,11},{10,... | collective-permute-start | bytes 73736 | tf_op jit(solution)/shard_map/ppermute | solution.py:41
  8.4 8.8 %collective-permute-start.2 = (f32[33,2,8,128]{3,2,1,0:T(8,128)S(1)}, f32[33,2,8,128]{3,2,1,0:T(8,128)S(1)}, u32[]{:S(2)}, u32[]{:S(2)}) collective-permute-start(f32[33,2,8,128]{3,2,1,0:T(8,128)S(1)} %get-tuple-element.32.kept_ref), channel_id=1, source_target_pairs={{0,16},{8,24},{16,0},{24,8},{1,17},{9,25},{17,1},{25,9},{2,18},{10... | collective-permute-start | bytes 811016 | tf_op jit(solution)/shard_map/ppermute | solution.py:41
  9.7 3.5 %collective-permute-start.4 = (f32[3,8,128]{2,1,0:T(8,128)S(1)}, f32[3,8,128]{2,1,0:T(8,128)S(1)}, u32[]{:S(2)}, u32[]{:S(2)}) collective-permute-start(f32[3,8,128]{2,1,0:T(8,128)S(1)} %get-tuple-element.36.own_ref), channel_id=1, source_target_pairs={{0,4},{1,5},{2,6},{3,7},{4,0},{5,1},{6,2},{7,3},{8,12},{9,13},{10,... | collective-permute-start | bytes 36872 | tf_op jit(solution)/shard_map/ppermute | solution.py:41
  13.2 5.0 %collective-permute-start.5 = (f32[1,2,3,8,128]{4,3,2,1,0:T(8,128)S(1)}, f32[1,2,3,8,128]{4,3,2,1,0:T(8,128)S(1)}, u32[]{:S(2)}, u32[]{:S(2)}) collective-permute-start(f32[1,2,3,8,128]{4,3,2,1,0:T(8,128)S(1)} %join.1.rest_3_), channel_id=1, source_target_pairs={{0,24},{8,16},{16,8},{24,0},{1,25},{9,17},{17,9},{25,1},{2,26},{10... | collective-permute-start | bytes 73736 | tf_op jit(solution)/shard_map/ppermute | solution.py:41
  16.8 2.7 %collective-permute-start.6 = (f32[1,2,3,8,128]{4,3,2,1,0:T(8,128)S(1)}, f32[1,2,3,8,128]{4,3,2,1,0:T(8,128)S(1)}, u32[]{:S(2)}, u32[]{:S(2)}) collective-permute-start(f32[1,2,3,8,128]{4,3,2,1,0:T(8,128)S(1)} %join.1.rest_3_), channel_id=1, source_target_pairs={{0,16},{8,24},{16,0},{24,8},{1,17},{9,25},{17,1},{25,9},{2,18},{10... | collective-permute-start | bytes 73736 | tf_op jit(solution)/shard_map/ppermute | solution.py:41
  16.8 2.7 %collective-permute-start.7 = (f32[1,2,3,8,128]{4,3,2,1,0:T(8,128)S(1)}, f32[1,2,3,8,128]{4,3,2,1,0:T(8,128)S(1)}, u32[]{:S(2)}, u32[]{:S(2)}) collective-permute-start(f32[1,2,3,8,128]{4,3,2,1,0:T(8,128)S(1)} %join.1.rest_3_), channel_id=1, source_target_pairs={{0,8},{8,0},{16,24},{24,16},{1,9},{9,1},{17,25},{25,17},{2,10},{10... | collective-permute-start | bytes 73736 | tf_op jit(solution)/shard_map/ppermute | solution.py:41

commit v7 on v6

--- a/solution.py
+++ b/solution.py
@@ -286,7 +286,10 @@
     place = lax.axis_index("az")
     lane = iota((fields, lanes), 1)
     for at, part in zip(reversed(starts), rest):
-        ghosts_ref[at : at + part.shape[0]] = part[:, :, tiles]
+        for i in range(part.shape[0]):
+            packed = part[i, 2 * tiles]
+            ghosts_ref[at + i, 0] = packed
+            ghosts_ref[at + i, 1] = pltpu.roll(packed, lanes // 2, 1)
     for at, part in zip(reversed(starts), rest):
         for i in range(part.shape[0]):
             own = place ^ (at + i)
@@ -295,8 +298,8 @@
             for e in range(2):
                 low = jnp.where(lane == 0, ghosts_ref[before, e], 0.0)
                 high = jnp.where(lane == lanes - 1, ghosts_ref[after, e], 0.0)
-                forcing_ref[at + i, e, 0] = part[i, e, 0] + low
-                forcing_ref[at + i, e, 1] = part[i, e, 1] + high
+                forcing_ref[at + i, e, 0] = part[i, tiles * e] + low
+                forcing_ref[at + i, e, 1] = part[i, tiles * e + 1] + high
     copies = []
     for batch in range(0, rows, BATCH):
         values = []
@@ -383,13 +386,20 @@
 
 
 def join_kernel(own_ref, other_ref, coeffs_ref, sums_ref, out_ref):
+    tiles = own_ref.shape[0] - 1
+    ghosts = []
     for e in range(2):
-        for t in range(own_ref.shape[0]):
-            out_ref[0, e, t] = (
+        for t in range(tiles + 1):
+            value = (
                 sums_ref[e, t]
                 + coeffs_ref[2 * e] * other_ref[t]
                 + coeffs_ref[2 * e + 1] * own_ref[t]
             )
+            if t < tiles:
+                out_ref[0, tiles * e + t] = value
+            else:
+                ghosts.append(value)
+    out_ref[0, 2 * tiles] = ghosts[0] + pltpu.roll(ghosts[1], LANES // 2, 1)
 
 
 def per_device(state, velocity, coupling, diffusivity, inverse, shifts):
@@ -465,7 +475,7 @@
         held, sums = merge(level, held, coeffs, sums)
     forcing = pl.pallas_call(
         join_kernel,
-        out_shape=pltpu.VMEM((1,) + sums.shape, f32),
+        out_shape=pltpu.VMEM((1, 2 * tiles + 1, fields, LANES), f32),
         in_specs=[VMEM] * 4,
         out_specs=VMEM,
         cost_estimate=cost(400),

time: 20.6 us -> 20.6 us (level)
  no operation moved by 1% of the time
where the time goes in v7:
time: 20.6 us; the launch traced here: 20.4 us
  starting transfers between devices  12.9 us (63%)
  Pallas kernels  4.62 us (22%)
  waiting for transfers between devices  2.86 us (14%)
    ppermute x8, starting transfers between devices, swapped(): lax.ppermute(block, axis, [(i, i ^ bit) for i in range(lax.axis_size(axis...  12.9 us
    ppermute x8, waiting for transfers between devices, swapped(): lax.ppermute(block, axis, [(i, i ^ bit) for i in range(lax.axis_size(axis...  2.86 us
    pallas_call x1, Pallas kernels, per_device(): pl.pallas_call(offsets_kernel, out_shape=[pltpu.VMEM((2, tiles + 1, field...  1.47 us
    pallas_call x1, Pallas kernels, per_device(): pl.pallas_call(functools.partial(solve_kernel, count, segments), out_shap...  1.47 us
    pallas_call x1, Pallas kernels, per_device(): pl.pallas_call(functools.partial(finish_kernel, count, starts), out_shape...  1.03 us
    pallas_call x1, Pallas kernels, per_device(): pl.pallas_call(functools.partial(rotate_kernel, count, bit), out_shape=pl...  0.44 us
  transfers between devices with their start and end apart: 8, of which 3 were waited for; matrix products, arithmetic and copies ran while one was open for 0% of the time, Pallas kernels for 10%

profile of v7, /device:TPU:1, one launch (start us, length us, event | category | flops | bytes accessed | tf_op | source)
XLA Modules:
  0.0 20.4 jit_solution(45732546018935311)
XLA Ops:
  0.0 0.0 copy-start
  0.0 1.5 %offsets.1 = (f32[2,3,8,128]{3,2,1,0:T(8,128)S(1)}, f32[8,32,256]{2,1,0:T(8,128)S(1)}, f32[1,32]{1,0:T(1,128)S(1)}, f32[1,8]{1,0:T(1,128)S(1)}, s32[32]{0:T(128)S(4)}, /*index=5*/f32[8,8]{1,0:T(8,128)S(4)}) custom-call(f32[8,32,256]{2,1,0:T(8,128)} %bitcast.6, f32[8,32,32]{2,1,0:T(8,128)} %inverse_ref.1, f32[1,32]{1,0:T(1,128)} %bitcast.7, ...), custom_call_target="tpu_custom_call" | custom-call | flops 1310720000 | bytes 5120000 | tf_op jit(solution)/shard_map/offsets/pallas_call | solution.py:412
  1.5 2.1 %collective-permute-start = (f32[2,3,8,128]{3,2,1,0:T(8,128)S(1)}, f32[2,3,8,128]{3,2,1,0:T(8,128)S(1)}, u32[]{:S(2)}, u32[]{:S(2)}) collective-permute-start(f32[2,3,8,128]{3,2,1,0:T(8,128)S(1)} %get-tuple-element.28.refs_0_), channel_id=1, source_target_pairs={{0,1},{1,0},{2,3},{3,2},{4,5},{5,4},{6,7},{7,6},{8,9},{9,8},{10,11... | collective-permute-start | bytes 73736 | tf_op jit(solution)/shard_map/ppermute | solution.py:41
  3.6 0.0 copy-done
  3.6 1.5 %solve.1 = (f32[33,2,8,128]{3,2,1,0:T(8,128)S(1)}, f32[2,32,8,128]{3,2,1,0:T(8,128)S(1)}, f32[14,8,128]{2,1,0:T(8,128)S(1)}, f32[4,8,128]{2,1,0:T(8,128)S(1)}) custom-call(f32[8,8]{1,0:T(8,128)S(4)} %get-tuple-element.23.coupling_ref, f32[8,32,256]{2,1,0:T(8,128)S(1)} %get-tuple-element.24.state_ref, f32[1,32]{1,0:T(1,128)S(1)} %get-tuple-element.25.velocity_ref, ...), custom_call_target="tpu_custom_call" | custom-call | flops 2097152000 | bytes 8192000 | tf_op jit(solution)/shard_map/solve/pallas_call | solution.py:435
  5.1 0.0 collective-permute-done.refs_1_
  5.1 1.3 %collective-permute-start.1 = (f32[33,2,8,128]{3,2,1,0:T(8,128)S(1)}, f32[33,2,8,128]{3,2,1,0:T(8,128)S(1)}, u32[]{:S(2)}, u32[]{:S(2)}) collective-permute-start(f32[33,2,8,128]{3,2,1,0:T(8,128)S(1)} %get-tuple-element.31.kept_ref), channel_id=1, source_target_pairs={{0,8},{8,0},{16,24},{24,16},{1,9},{9,1},{17,25},{25,17},{2,10},{10... | collective-permute-start | bytes 811016 | tf_op jit(solution)/shard_map/ppermute | solution.py:41
  6.4 1.8 %collective-permute-start.3 = (f32[2,3,8,128]{3,2,1,0:T(8,128)S(1)}, f32[2,3,8,128]{3,2,1,0:T(8,128)S(1)}, u32[]{:S(2)}, u32[]{:S(2)}) collective-permute-start(f32[2,3,8,128]{3,2,1,0:T(8,128)S(1)} %get-tuple-element.33.refs_0_), channel_id=1, source_target_pairs={{0,2},{1,3},{2,0},{3,1},{4,6},{5,7},{6,4},{7,5},{8,10},{9,11},{10,... | collective-permute-start | bytes 73736 | tf_op jit(solution)/shard_map/ppermute | solution.py:41
  8.3 0.0 collective-permute-done.1.came_ref
  8.3 0.1 select.1
  8.4 1.3 %collective-permute-start.2 = (f32[33,2,8,128]{3,2,1,0:T(8,128)S(1)}, f32[33,2,8,128]{3,2,1,0:T(8,128)S(1)}, u32[]{:S(2)}, u32[]{:S(2)}) collective-permute-start(f32[33,2,8,128]{3,2,1,0:T(8,128)S(1)} %get-tuple-element.32.kept_ref), channel_id=1, source_target_pairs={{0,16},{8,24},{16,0},{24,8},{1,17},{9,25},{17,1},{25,9},{2,18},{10... | collective-permute-start | bytes 811016 | tf_op jit(solution)/shard_map/ppermute | solution.py:41
  9.7 0.0 collective-permute-done.3.refs_1_
  9.7 2.4 %collective-permute-start.4 = (f32[3,8,128]{2,1,0:T(8,128)S(1)}, f32[3,8,128]{2,1,0:T(8,128)S(1)}, u32[]{:S(2)}, u32[]{:S(2)}) collective-permute-start(f32[3,8,128]{2,1,0:T(8,128)S(1)} %get-tuple-element.36.own_ref), channel_id=1, source_target_pairs={{0,4},{1,5},{2,6},{3,7},{4,0},{5,1},{6,2},{7,3},{8,12},{9,13},{10,... | collective-permute-start | bytes 36872 | tf_op jit(solution)/shard_map/ppermute | solution.py:41
  12.1 1.1 %collective-permute-done.4.other_ref = f32[3,8,128]{2,1,0:T(8,128)S(1)} collective-permute-done((f32[3,8,128]{2,1,0:T(8,128)S(1)}, f32[3,8,128]{2,1,0:T(8,128)S(1)}, u32[]{:S(2)}, u32[]{:S(2)}) %collective-permute-start.4) | collective-permute-done | bytes 12320 | tf_op jit(solution)/shard_map/ppermute | solution.py:41
  13.2 0.1 join.1.rest_3_
  13.3 3.5 %collective-permute-start.5 = (f32[1,5,8,128]{3,2,1,0:T(8,128)S(1)}, f32[1,5,8,128]{3,2,1,0:T(8,128)S(1)}, u32[]{:S(2)}, u32[]{:S(2)}) collective-permute-start(f32[1,5,8,128]{3,2,1,0:T(8,128)S(1)} %join.1.rest_3_), channel_id=1, source_target_pairs={{0,24},{8,16},{16,8},{24,0},{1,25},{9,17},{17,9},{25,1},{2,26},{10... | collective-permute-start | bytes 61448 | tf_op jit(solution)/shard_map/ppermute | solution.py:41
  16.8 0.0 collective-permute-start.6
  16.8 0.5 %collective-permute-start.7 = (f32[1,5,8,128]{3,2,1,0:T(8,128)S(1)}, f32[1,5,8,128]{3,2,1,0:T(8,128)S(1)}, u32[]{:S(2)}, u32[]{:S(2)}) collective-permute-start(f32[1,5,8,128]{3,2,1,0:T(8,128)S(1)} %join.1.rest_3_), channel_id=1, source_target_pairs={{0,8},{8,0},{16,24},{24,16},{1,9},{9,1},{17,25},{25,17},{2,10},{10... | collective-permute-start | bytes 61448 | tf_op jit(solution)/shard_map/ppermute | solution.py:41
  17.2 0.0 collective-permute-done.2.came_ref
  17.2 0.4 %rotate.1.rotated_ref = f32[32,2,8,128]{3,2,1,0:T(8,128)S(1)} custom-call(s32[32]{0:T(128)S(4)} %get-tuple-element.22.shifts_ref, f32[33,2,8,128]{3,2,1,0:T(8,128)S(1)} %get-tuple-element.32.kept_ref, f32[33,2,8,128]{3,2,1,0:T(8,128)S(1)} %collective-permute-done.2.came_ref), custom_call_target="tpu_custom_call" | custom-call | flops 1048576000 | bytes 4096000 | tf_op jit(solution)/shard_map/rotate/pallas_call | solution.py:465
  17.7 0.5 %collective-permute-done.5.rest_0_ = f32[1,5,8,128]{3,2,1,0:T(8,128)S(1)} collective-permute-done((f32[1,5,8,128]{3,2,1,0:T(8,128)S(1)}, f32[1,5,8,128]{3,2,1,0:T(8,128)S(1)}, u32[]{:S(2)}, u32[]{:S(2)}) %collective-permute-start.5) | collective-permute-done | bytes 20512 | tf_op jit(solution)/shard_map/ppermute | solution.py:41
  18.2 1.2 %collective-permute-done.6.rest_1_ = f32[1,5,8,128]{3,2,1,0:T(8,128)S(1)} collective-permute-done((f32[1,5,8,128]{3,2,1,0:T(8,128)S(1)}, f32[1,5,8,128]{3,2,1,0:T(8,128)S(1)}, u32[]{:S(2)}, u32[]{:S(2)}) %collective-permute-start.6) | collective-permute-done | bytes 20512 | tf_op jit(solution)/shard_map/ppermute | solution.py:41
  19.4 0.0 collective-permute-done.7.rest_2_
  19.4 1.0 %finish.1 = f32[8,32,256]{2,1,0:T(8,128)} custom-call(s32[32]{0:T(128)S(4)} %get-tuple-element.22.shifts_ref, f32[2,32,8,128]{3,2,1,0:T(8,128)S(1)} %get-tuple-element.27.columns_ref, f32[32,2,8,128]{3,2,1,0:T(8,128)S(1)} %rotate.1.rotated_ref, f32[1,5,8,128]{3,2,1,0:T(8,128)S(1)} %collective-permute-done.5.rest_0_, ...), custom_call_target="tpu_custom_call" | custom-call | flops 1572864000 | bytes 6144000 | tf_op jit(solution)/shard_map/finish/pallas_call | solution.py:491
  (2 shorter events, 0.0 us)
Async XLA Ops:
  0.0 3.6 %copy-start = (f32[8,32,32]{2,1,0:T(8,128)S(1)}, f32[8,32,32]{2,1,0:T(8,128)}, u32[]{:S(2)}) copy-start(f32[8,32,32]{2,1,0:T(8,128)} %inverse_ref.1) | copy-start | bytes 98308
  1.5 3.6 %collective-permute-start = (f32[2,3,8,128]{3,2,1,0:T(8,128)S(1)}, f32[2,3,8,128]{3,2,1,0:T(8,128)S(1)}, u32[]{:S(2)}, u32[]{:S(2)}) collective-permute-start(f32[2,3,8,128]{3,2,1,0:T(8,128)S(1)} %get-tuple-element.28.refs_0_), channel_id=1, source_target_pairs={{0,1},{1,0},{2,3},{3,2},{4,5},{5,4},{6,7},{7,6},{8,9},{9,8},{10,11... | collective-permute-start | bytes 73736 | tf_op jit(solution)/shard_map/ppermute | solution.py:41
  5.1 3.2 %collective-permute-start.1 = (f32[33,2,8,128]{3,2,1,0:T(8,128)S(1)}, f32[33,2,8,128]{3,2,1,0:T(8,128)S(1)}, u32[]{:S(2)}, u32[]{:S(2)}) collective-permute-start(f32[33,2,8,128]{3,2,1,0:T(8,128)S(1)} %get-tuple-element.31.kept_ref), channel_id=1, source_target_pairs={{0,8},{8,0},{16,24},{24,16},{1,9},{9,1},{17,25},{25,17},{2,10},{10... | collective-permute-start | bytes 811016 | tf_op jit(solution)/shard_map/ppermute | solution.py:41
  6.4 3.3 %collective-permute-start.3 = (f32[2,3,8,128]{3,2,1,0:T(8,128)S(1)}, f32[2,3,8,128]{3,2,1,0:T(8,128)S(1)}, u32[]{:S(2)}, u32[]{:S(2)}) collective-permute-start(f32[2,3,8,128]{3,2,1,0:T(8,128)S(1)} %get-tuple-element.33.refs_0_), channel_id=1, source_target_pairs={{0,2},{1,3},{2,0},{3,1},{4,6},{5,7},{6,4},{7,5},{8,10},{9,11},{10,... | collective-permute-start | bytes 73736 | tf_op jit(solution)/shard_map/ppermute | solution.py:41
  8.4 8.8 %collective-permute-start.2 = (f32[33,2,8,128]{3,2,1,0:T(8,128)S(1)}, f32[33,2,8,128]{3,2,1,0:T(8,128)S(1)}, u32[]{:S(2)}, u32[]{:S(2)}) collective-permute-start(f32[33,2,8,128]{3,2,1,0:T(8,128)S(1)} %get-tuple-element.32.kept_ref), channel_id=1, source_target_pairs={{0,16},{8,24},{16,0},{24,8},{1,17},{9,25},{17,1},{25,9},{2,18},{10... | collective-permute-start | bytes 811016 | tf_op jit(solution)/shard_map/ppermute | solution.py:41
  9.7 3.5 %collective-permute-start.4 = (f32[3,8,128]{2,1,0:T(8,128)S(1)}, f32[3,8,128]{2,1,0:T(8,128)S(1)}, u32[]{:S(2)}, u32[]{:S(2)}) collective-permute-start(f32[3,8,128]{2,1,0:T(8,128)S(1)} %get-tuple-element.36.own_ref), channel_id=1, source_target_pairs={{0,4},{1,5},{2,6},{3,7},{4,0},{5,1},{6,2},{7,3},{8,12},{9,13},{10,... | collective-permute-start | bytes 36872 | tf_op jit(solution)/shard_map/ppermute | solution.py:41
  13.3 4.9 %collective-permute-start.5 = (f32[1,5,8,128]{3,2,1,0:T(8,128)S(1)}, f32[1,5,8,128]{3,2,1,0:T(8,128)S(1)}, u32[]{:S(2)}, u32[]{:S(2)}) collective-permute-start(f32[1,5,8,128]{3,2,1,0:T(8,128)S(1)} %join.1.rest_3_), channel_id=1, source_target_pairs={{0,24},{8,16},{16,8},{24,0},{1,25},{9,17},{17,9},{25,1},{2,26},{10... | collective-permute-start | bytes 61448 | tf_op jit(solution)/shard_map/ppermute | solution.py:41
  16.8 2.6 %collective-permute-start.6 = (f32[1,5,8,128]{3,2,1,0:T(8,128)S(1)}, f32[1,5,8,128]{3,2,1,0:T(8,128)S(1)}, u32[]{:S(2)}, u32[]{:S(2)}) collective-permute-start(f32[1,5,8,128]{3,2,1,0:T(8,128)S(1)} %join.1.rest_3_), channel_id=1, source_target_pairs={{0,16},{8,24},{16,0},{24,8},{1,17},{9,25},{17,1},{25,9},{2,18},{10... | collective-permute-start | bytes 61448 | tf_op jit(solution)/shard_map/ppermute | solution.py:41
  16.8 2.6 %collective-permute-start.7 = (f32[1,5,8,128]{3,2,1,0:T(8,128)S(1)}, f32[1,5,8,128]{3,2,1,0:T(8,128)S(1)}, u32[]{:S(2)}, u32[]{:S(2)}) collective-permute-start(f32[1,5,8,128]{3,2,1,0:T(8,128)S(1)} %join.1.rest_3_), channel_id=1, source_target_pairs={{0,8},{8,0},{16,24},{24,16},{1,9},{9,1},{17,25},{25,17},{2,10},{10... | collective-permute-start | bytes 61448 | tf_op jit(solution)/shard_map/ppermute | solution.py:41
